TPU v7x, 32 devices: a whole 2x2x4 slice. The times are simulated.
32 devices in a mesh: dp: 16 (over z, y, x), tensor: 2 (over core).
Axes of the slice: x: 2, y: 2, z: 4, core: 2. Of those that a mesh axis runs over, the one named last changes fastest.
Arguments:
- tokens: bfloat16 [128, 185, 768], P('dp'), may hold values from -6 to 6
- cotangent: bfloat16 [128, 185, 768], P('dp'), may hold values from -6 to 6
- caption_lengths: int32 [128], P('dp'), may hold values from 5 to 40
- item_counts: int32 [16], P('dp'), may hold values from 1 to 8, as said below
- w_qkv: bfloat16 [768, 3, 768], P(None, None, 'tensor'), may hold values from -0.21875 to 0.21875
- qv_bias: float32 [2, 768], P(None, 'tensor'), may hold values from -2 to 2
- w_out: bfloat16 [768, 768], P('tensor'), may hold values from -0.625 to 0.625
- out_bias: float32 [768], replicated, may hold values from -2 to 2
- w_up: bfloat16 [768, 3072], P(None, 'tensor'), may hold values from -0.21875 to 0.21875
- up_bias: float32 [3072], P('tensor'), may hold values from -3 to 3
- w_down: bfloat16 [3072, 768], P('tensor'), may hold values from -0.109375 to 0.109375
- down_bias: float32 [768], replicated, may hold values from -2 to 2
- ln_gains: float32 [2, 768], replicated, may hold values from 0.5 to 1.5
- ln_biases: float32 [2, 768], replicated, may hold values from -2 to 2
Outputs:
- output: bfloat16 [128, 185, 768], P('dp')
- grad_tokens: bfloat16 [128, 185, 768], P('dp')
- grad_qkv: float32 [768, 3, 768], P(None, None, 'tensor')
- grad_qv_bias: float32 [2, 768], P(None, 'tensor')
- grad_out: float32 [768, 768], P('tensor')
- grad_out_bias: float32 [768], replicated
- grad_up: float32 [768, 3072], P(None, 'tensor')
- grad_up_bias: float32 [3072], P('tensor')
- grad_down: float32 [3072, 768], P('tensor')
- grad_down_bias: float32 [768], replicated
- grad_ln_gains: float32 [2, 768], replicated
- grad_ln_biases: float32 [2, 768], replicated
Inputs may be any that keep to these rules, and one draw needn't show every extreme that they name: `item_counts`: item slots of a device at or beyond its count hold no item; some device has 8 live slots and some has 1.
All inputs are finite; a program needn't handle non-finite values.
Results may differ from a plain program's by a relative error of at most 0.013.
Values sent between devices are 32-bit elements; how exact they have to be, the bound alone decides.
No kernel may reach another device: no remote copies, remote signals or barrier semaphores. Data moves between devices by JAX's collectives and lax.ppermute only.
A program may use at most 192 MiB of HBM per device.

v0:
```python
import jax
import jax.numpy as jnp
from jax import lax
from jax.experimental import pallas as pl
from jax.experimental.pallas import tpu as pltpu
from jax.sharding import PartitionSpec as P

HEAD_DIM = 64
PATCHES = 144
EPS = 1e-05
MIB = 1024 * 1024
COST = 1024
F32 = jnp.float32
BF16 = jnp.bfloat16


def mm(a, b, da=1, db=0):
    return lax.dot_general(a, b, (((da,), (db,)), ((), ())), preferred_element_type=F32)


def whole(shape):
    return pl.BlockSpec(shape, lambda *_: (0,) * len(shape))


def anywhere():
    return pl.BlockSpec(memory_space=pl.ANY)


def smem():
    return pl.BlockSpec(memory_space=pltpu.SMEM)


def in_hbm(v):
    return pltpu.with_memory_space_constraint(v, pltpu.HBM)


def here(v):
    return pltpu.with_memory_space_constraint(v, pltpu.VMEM)


class Order:
    def __init__(self):
        self.last = ()


def call(body, grid, ins, in_specs, outs, out_specs, scratch=(), aliases=None, order=None, vmem=24):
    n_in, n_out = len(ins), len(outs)

    def kernel(*refs):
        after_in = n_in + len(order.last)
        body(*refs[:n_in], *refs[after_in : after_in + n_out], *refs[after_in + n_out + 1 :])

    *res, token = pl.pallas_call(
        kernel,
        grid=grid,
        in_specs=list(in_specs) + [anywhere()] * len(order.last),
        out_specs=list(out_specs) + [anywhere()],
        out_shape=list(outs) + [pltpu.HBM((8, 128), F32)],
        scratch_shapes=list(scratch),
        input_output_aliases=aliases or {},
        compiler_params=pltpu.CompilerParams(vmem_limit_bytes=vmem * MIB),
        cost_estimate=pl.CostEstimate(flops=COST, bytes_accessed=COST, transcendentals=0),
    )(*ins, *[in_hbm(v) for v in order.last])
    order.last = (token,)
    return res


def sds(shape, dtype):
    return jax.ShapeDtypeStruct(shape, dtype)


def normed(v):
    centred = v - jnp.mean(v, axis=-1, keepdims=True)
    inverse = lax.rsqrt(jnp.mean(centred * centred, axis=-1, keepdims=True) + EPS)
    return centred * inverse, inverse


def norm_back(e, n, inverse, gain):
    eg = e * gain
    return inverse * (
        eg - jnp.mean(eg, axis=-1, keepdims=True) - n * jnp.mean(eg * n, axis=-1, keepdims=True)
    )


def colsum(v):
    return jnp.sum(v, axis=0, keepdims=True)


def in_vmem():
    return pl.BlockSpec(memory_space=pltpu.VMEM)


BITS = {"x": 0, "y": 1, "a": 2, "b": 3}
HALVING = ("x", "y", "a", "b")


hbm = pltpu.HBM
vmem = pltpu.VMEM


class Links:
    def __init__(self, n_dp, n_t):
        self.n_dp, self.n_t = n_dp, n_t
        self.extra = tuple(range(4, n_dp.bit_length() - 1))

    def swap(self, v, dims):
        pairs = [
            (d * self.n_t + t, (d ^ (1 << BITS.get(dims[t % 2], dims[t % 2]))) * self.n_t + t)
            for d in range(self.n_dp)
            for t in range(self.n_t)
        ]
        return lax.ppermute(v, ("dp", "tensor"), pairs)

    def table(self):
        d, t = lax.axis_index("dp"), lax.axis_index("tensor") % 2
        return [
            ((d >> jnp.where(t == 0, BITS[v], BITS[w])) & 1).reshape(1) for v in HALVING for w in HALVING
        ]

    def place(self, dims):
        return HALVING.index(dims[0]) * 4 + HALVING.index(dims[1])


def add_split(keep, got, side_of, order):
    n, width = keep.shape
    h = n // 2

    def body(b_ref, k_ref, r_ref, ko_ref, so_ref):
        side = b_ref[0]
        mine = pl.ds(pl.multiple_of(side * h, 8), h)
        rest = pl.ds(pl.multiple_of((1 - side) * h, 8), h)
        so_ref[...] = k_ref[rest, :] + r_ref[rest, :]
        ko_ref[...] = k_ref[mine, :] + r_ref[mine, :]

    return call(
        body, (), [side_of, keep, got], [smem(), in_vmem(), in_vmem()],
        [sds((h, width), F32)] * 2, [in_vmem()] * 2, order=order, vmem=5,
    )


def add(keep, got, order):
    def body(k_ref, r_ref, o_ref):
        o_ref[...] = k_ref[...] + r_ref[...]

    return call(
        body, (), [keep, got], [in_vmem()] * 2, [sds(keep.shape, F32)], [in_vmem()], order=order, vmem=5
    )[0]


def join(mine, got, side_of, order):
    n, width = mine.shape

    def body(b_ref, m_ref, r_ref, o_ref):
        side = b_ref[0]
        o_ref[pl.ds(pl.multiple_of(side * n, 8), n), :] = m_ref[...]
        o_ref[pl.ds(pl.multiple_of((1 - side) * n, 8), n), :] = r_ref[...]

    return call(
        body, (), [side_of, mine, got], [smem(), in_vmem(), in_vmem()],
        [sds((2 * n, width), F32)], [in_vmem()], order=order, vmem=5,
    )[0]


class Piece:
    def __init__(self, links, sides, dims, keep, send, finish):
        self.links, self.sides, self.finish = links, sides, finish
        *halving, last = zip(*dims)
        whole = [last] + [(e, e) for e in links.extra]
        self.stages = (
            [(d, "half") for d in halving] + [(d, "whole") for d in whole] + [(d, "back") for d in halving[::-1]]
        )
        self.at = 0
        self.keep = keep
        self.got = links.swap(send, halving[0])

    def step(self, order):
        dim, kind = self.stages[self.at]
        self.at += 1
        if self.at == len(self.stages):
            self.finish(self.keep, self.got, order)
            return
        following, next_kind = self.stages[self.at]
        if kind == "back":
            self.keep = send = join(self.keep, self.got, self.sides[self.links.place(dim)], order)
        elif next_kind == "half":
            self.keep, send = add_split(self.keep, self.got, self.sides[self.links.place(following)], order)
        else:
            self.keep = send = add(self.keep, self.got, order)
        self.got = self.links.swap(send, following)


def on_device(
    links,
    plan,
    tokens,
    cotangent,
    caption_lengths,
    item_counts,
    w_qkv,
    qv_bias,
    w_out,
    out_bias,
    w_up,
    up_bias,
    w_down,
    down_bias,
    ln_gains,
    ln_biases,
):
    order = Order()
    sides = links.table()
    first = [sides[links.place((v[0][0], v[1][0]))] for v in plan["dims"]]
    items, seq, D = tokens.shape
    W = w_qkv.shape[2]
    FL = w_up.shape[1]
    pairs = W // 128
    heads = W // HEAD_DIM
    SP = -(-seq // 64) * 64
    R = items * SP
    IB = 2
    BR = IB * SP
    steps = items // IB
    scale = HEAD_DIM ** (-0.5)

    wq = jnp.transpose(w_qkv, (1, 0, 2))
    bias3 = jnp.concatenate([qv_bias[0], jnp.zeros((W,), F32), qv_bias[1]]).reshape(1, 3 * W)
    g1, g2 = ln_gains[0:1], ln_gains[1:2]
    b1, b2 = ln_biases[0:1], ln_biases[1:2]
    out_b = out_bias.reshape(1, D)
    down_b = down_bias.reshape(1, D)
    up_b = up_bias.reshape(1, FL)
    by_token = (1, 0, 2)
    state = {}
    pieces = {}
    up_sums = []
    swap = [(0, 1), (1, 0)]

    def other(v):
        return lax.ppermute(v, "tensor", swap)

    rowD = pl.BlockSpec((BR, D), lambda t: (t, 0))
    rowW = pl.BlockSpec((BR, W), lambda t: (t, 0))
    row3 = pl.BlockSpec((BR, 3 * W), lambda t: (t, 0))

    def release(arrays, space):
        n = len(arrays)
        return call(
            lambda *refs: None,
            (),
            [pltpu.with_memory_space_constraint(v, space) for v in arrays],
            [anywhere()] * n,
            [space(v.shape, v.dtype) for v in arrays],
            [anywhere()] * n,
            aliases={i: i for i in range(n)},
            order=order,
            vmem=4,
        )

    def dc_send():
        state["dc"] = release([state["dc"]], vmem)[0]
        state["dc_got"] = other(state["dc"])

    def da_send():
        state["da"] = release([state["da"]], vmem)[0]
        state["da_got"] = other(state["da"])

    def y_send():
        state["y"] = release([state["y"]], vmem)[0]
        state["y_got"] = other(state["y"])

    def spread(name, source, masked):
        def body(cnt_ref, *rest):
            t_ref, o_ref, sum_ref, xs = rest[-4:]
            for k in range(D // 128):
                cols = pl.ds(k * 128, 128)
                xs[k, pl.ds(0, seq * items), :] = t_ref[:, :, cols].astype(F32).reshape(seq * items, 128)
                xs[k, pl.ds(seq * items, (SP - seq) * items), :] = jnp.zeros(((SP - seq) * items, 128), F32)
                total = jnp.zeros((1, 128), F32)
                for i in range(items):
                    v = xs[k, pl.ds(i, SP, stride=items), :]
                    if masked:
                        v = jnp.where(i < cnt_ref[0], v, 0.0)
                        total = total + colsum(v)
                    o_ref[pl.ds(i * SP, SP), cols] = v.astype(BF16)
                sum_ref[:, cols] = total

        state[name], state[name + "_sum"] = call(
            body,
            (),
            [item_counts, *sides, jnp.transpose(source, by_token)],
            [smem()] * (1 + len(sides)) + [in_vmem()],
            [vmem((R, D), BF16), sds((1, D), F32)],
            [in_vmem()] * 2,
            [pltpu.VMEM((D // 128, SP * items, 128), F32)],
            order=order,
            vmem=8,
        )

    IH = items // 2
    RH = R // 2

    def attn_fwd(half):
        off = half * RH
        names = ("a", "qkv", "pr", "ctx", "x_kept")

        def body(len_ref, x_ref, wq_ref, b3_ref, g_ref, b_ref, wo_ref, *rest):
            part_ref, a_out, qkv_out, pr_out, ctx_out, x_out, a_ref, qkv_ref, pr_ref, ctx_ref, sems = rest[-11:]
            mine = pl.ds(off, RH)
            copies = []

            def copy_out(source, target):
                copy = pltpu.make_async_copy(source, target, sems.at[len(copies)])
                copy.start()
                copies.append(copy)

            copy_out(x_ref.at[mine], x_out.at[mine])
            n, _ = normed(x_ref[mine, :].astype(F32))
            a = (n * g_ref[...] + b_ref[...]).astype(BF16)
            a_ref[...] = a
            copy_out(a_ref, a_out.at[mine])
            for c in range(3):
                cols = pl.ds(c * W, W)
                qkv_ref[:, cols] = (mm(a, wq_ref[c]) + b3_ref[:, cols]).astype(BF16)
            copy_out(qkv_ref, qkv_out.at[mine])
            lane = lax.broadcasted_iota(jnp.int32, (SP, 128), 1)
            key_at = lax.broadcasted_iota(jnp.int32, (SP, SP), 0)
            zero = jnp.zeros((SP, 128), BF16)
            for i in range(IH):
                valid = key_at < PATCHES + 1 + len_ref[half * IH + i]
                rows = pl.ds(i * SP, SP)
                for j in range(pairs):
                    q = qkv_ref[rows, pl.ds(j * 128, 128)] * jnp.asarray(scale, BF16)
                    k = qkv_ref[rows, pl.ds(W + j * 128, 128)]
                    v = qkv_ref[rows, pl.ds(2 * W + j * 128, 128)]
                    ctx = None
                    for s in range(2):
                        side = (lane < 64) if s == 0 else (lane >= 64)
                        st = mm(k, jnp.where(side, q, zero), 1, 1)
                        st = jnp.where(valid, st, -1e30)
                        e = jnp.exp(st - jnp.max(st, axis=0, keepdims=True))
                        pr = (e * (1.0 / jnp.sum(e, axis=0, keepdims=True))).astype(BF16)
                        pr_ref[i, 2 * j + s] = pr
                        c = mm(pr, jnp.where(side, v, zero), 0, 0)
                        ctx = c if ctx is None else ctx + c
                    ctx_ref[rows, pl.ds(j * 128, 128)] = ctx.astype(BF16)
                copy_out(pr_ref.at[i], pr_out.at[half * IH + i])
            copy_out(ctx_ref, ctx_out.at[mine])
            part_ref[...] = mm(ctx_ref[...], wo_ref[...])
            for copy in copies:
                copy.wait()

        ins = [caption_lengths, here(state["x"]), wq, bias3, g1, b1, w_out]
        specs = [smem()] + [in_vmem()] * 6
        outs = [
            vmem((RH, D), F32),
            hbm((R, D), BF16),
            hbm((R, 3 * W), BF16),
            hbm((items, heads, SP, SP), BF16),
            hbm((R, W), BF16),
            hbm((R, D), BF16),
        ]
        aliases = {}
        if half:
            aliases = {len(ins) + n: 1 + n for n in range(5)}
            ins += [in_hbm(state[v]) for v in names]
            specs += [anywhere()] * 5
        part, *kept = call(
            body,
            (),
            ins,
            specs,
            outs,
            [in_vmem()] + [anywhere()] * 5,
            [
                pltpu.VMEM((RH, D), BF16),
                pltpu.VMEM((RH, 3 * W), BF16),
                pltpu.VMEM((IH, heads, SP, SP), BF16),
                pltpu.VMEM((RH, W), BF16),
                pltpu.SemaphoreType.DMA((4 + IH,)),
            ],
            aliases,
            order=order,
            vmem=16,
        )
        state.update(zip(names, kept))
        return part

    spread("x", tokens, False)
    parts, got = [], []
    for half in range(2):
        part = attn_fwd(half)
        parts.append(part)
        got.append(other(part))

    def second(half):
        def body(x_ref, p_ref, r_ref, ob_ref, g_ref, b_ref, *rest):
            h_ref, c_ref, ct_ref = rest[-3:]
            h = x_ref[...].astype(F32) + (p_ref[...] + r_ref[...]) + ob_ref[...]
            h_ref[...] = h.astype(BF16)
            n, _ = normed(h)
            c = (n * g_ref[...] + b_ref[...]).astype(BF16)
            c_ref[...] = c
            ct_ref[...] = c.T

        off = half * (steps // 2)
        row = lambda t: (t + off, 0)
        ins = [state["x"], parts[half], got[half], out_b, g2, b2]
        specs = [pl.BlockSpec((BR, D), row), rowD, rowD, in_vmem(), in_vmem(), in_vmem()]
        outs = [vmem((R, D), BF16), vmem((R, D), BF16), vmem((D, R), BF16)]
        out_specs = [
            pl.BlockSpec((BR, D), row),
            pl.BlockSpec((BR, D), row),
            pl.BlockSpec((D, BR), lambda t: (0, t + off)),
        ]
        names = ("h", "c", "ct")
        aliases = {}
        if half:
            aliases = {len(ins) + n: n for n in range(3)}
            ins += [here(state["h"]), here(state["c"]), here(state["ct"])]
            specs += [anywhere()] * 3
        kept = call(
            body, (steps // 2,), ins, specs, outs, out_specs, (), aliases, order=order, vmem=11
        )
        state.update(zip(names, kept))

    second(0)
    spread("dy", cotangent, True)
    second(1)

    sizes = [128 * v for v in plan["units"]]
    chunks = len(sizes)
    starts = [sum(sizes[:f]) for f in range(chunks)]
    SB = 256
    DH = D // 2
    HL = FL // 2
    blocks = DH // 128

    def ffn(f):
        HU = sizes[f]
        FC = 2 * HU

        def body(p_ref, c_ref, ct_ref, dy_ref, wu_ref, ub_ref, wd_ref, keep_ref, send_ref, sum_ref, r_ref, du_ref, acc):
            p = p_ref[0]
            units = [pl.ds(starts[f] + side * HL, HU) for side in range(2)]
            wu = jnp.concatenate([wu_ref[:, v] for v in units], axis=1)
            wd = jnp.concatenate([wd_ref[v, :] for v in units], axis=0)
            ub = jnp.concatenate([ub_ref[:, v] for v in units], axis=1)
            total = jnp.zeros((1, FC), F32)
            for s in range(R // SB):
                rows = pl.ds(s * SB, SB)
                u = mm(c_ref[rows, :], wu) + ub
                dr = mm(dy_ref[rows, :], wd, 1, 1)
                below = 0.5 + 0.5 * lax.erf(u * (0.5**0.5))
                density = jnp.exp(-0.5 * u * u) * 0.3989422804014327
                r_ref[rows, :] = (u * below).astype(BF16)
                du = (dr * (below + u * density)).astype(BF16)
                du_ref[rows, :] = du
                total = total + colsum(du.astype(F32))
            sum_ref[...] = total
            gd = mm(r_ref[...], dy_ref[...], 0, 0)
            for half in range(2):
                acc[half, pl.ds(0, HU), :] = gd[half * HU : (half + 1) * HU]
            gu = mm(ct_ref[...], du_ref[...])
            for half in range(2):
                for j in range(HU // 128):
                    for b in range(blocks):
                        for side in range(2):
                            acc[half, pl.ds(HU + j * 128, 128), pl.ds((2 * b + side) * 128, 128)] = gu[
                                half * DH + b * 128 : half * DH + (b + 1) * 128,
                                side * HU + j * 128 : side * HU + (j + 1) * 128,
                            ]
            keep_ref[...] = acc[p]
            send_ref[...] = acc[1 - p]

        keep, send, total, state["r", f], state["du", f] = call(
            body,
            (),
            [first[f], here(state["c"]), here(state["ct"]), here(state["dy"]), w_up, up_b, w_down],
            [smem()] + [in_vmem()] * 6,
            [
                vmem((FC, D), F32),
                vmem((FC, D), F32),
                sds((1, FC), F32),
                vmem((R, FC), BF16),
                vmem((R, FC), BF16),
            ],
            [in_vmem()] * 5,
            [pltpu.VMEM((2, FC, D), F32)],
            order=order,
            vmem=10,
        )
        up_sums.append(total)

        def finish(mine, got, order):
            def body(p_ref, m_ref, g_ref, *rest):
                gd_ref, gu_ref = rest[-2:]
                own = pl.program_id(0) == p_ref[0]

                def write(ref, side):
                    gd_ref[...] = ref[pl.ds(0, HU), :]
                    for j in range(HU // 128):
                        for b in range(blocks):
                            gu_ref[pl.ds(b * 128, 128), pl.ds(j * 128, 128)] = ref[
                                pl.ds(HU + j * 128, 128), pl.ds((2 * b + side) * 128, 128)
                            ]

                for side in range(2):
                    this = pl.program_id(1) == side

                    @pl.when(own & this)
                    def _(side=side):
                        write(m_ref, side)

                    @pl.when(jnp.logical_not(own) & this)
                    def _(side=side):
                        write(g_ref, side)

            ins, specs, aliases = [first[f], mine, got], [smem(), in_vmem(), in_vmem()], {}
            if "gd" in state:
                aliases = {3: 0, 4: 1}
                ins += [in_hbm(state["gd"]), in_hbm(state["gu"])]
                specs += [anywhere()] * 2
            state["gd"], state["gu"] = call(
                body,
                (2, 2),
                ins,
                specs,
                [hbm((FL, D), F32), hbm((D, FL), F32)],
                [
                    pl.BlockSpec((HU, D), lambda t, s: ((t * HL + starts[f]) // HU, 0)),
                    pl.BlockSpec((DH, HU), lambda t, s: (t, (s * HL + starts[f]) // HU)),
                ],
                aliases=aliases,
                order=order,
                vmem=10,
            )

        pieces[f] = Piece(links, sides, plan["dims"][f], keep, send, finish)

    def in_order(refs):
        return jnp.concatenate(
            [ref[:, pl.ds(side * hu, hu)] for side in range(2) for ref, hu in zip(refs, sizes)], axis=1
        )

    def dc():
        def body(*refs):
            refs[-1][...] = mm(in_order(refs[:-2]), refs[-2][...], 1, 1)

        rowF = [pl.BlockSpec((BR, 2 * hu), lambda t: (t, 0)) for hu in sizes]
        (state["dc"],) = call(
            body,
            (steps,),
            [here(state["du", f]) for f in range(chunks)] + [w_up],
            rowF + [in_vmem()],
            [vmem((R, D), F32)],
            [rowD],
            order=order,
            vmem=6,
        )

    def y():
        def body(*refs):
            refs[-1][...] = mm(in_order(refs[:-2]), refs[-2][...])

        rowF = [pl.BlockSpec((BR, 2 * hu), lambda t: (t, 0)) for hu in sizes]
        (state["y"],) = call(
            body,
            (steps,),
            [here(state["r", f]) for f in range(chunks)] + [w_down],
            rowF + [in_vmem()],
            [vmem((R, D), F32)],
            [rowD],
            order=order,
            vmem=8,
        )

    def back2():
        def body(h_ref, dy_ref, ctx_ref, wo_ref, g_ref, e0_ref, e1_ref, dh_ref, dctx_ref, go_ref, sum_ref):
            step = pl.program_id(0)
            e = e0_ref[...] + e1_ref[...]
            n, inverse = normed(h_ref[...].astype(F32))
            dh = dy_ref[...].astype(F32) + norm_back(e, n, inverse, g_ref[...])
            dhr = dh.astype(BF16)
            dh_ref[...] = dhr
            dctx_ref[...] = mm(dhr, wo_ref[...], 1, 1).astype(BF16)
            sum_ref[0, 0:1] = colsum(e * n)
            sum_ref[0, 1:2] = colsum(e)
            sum_ref[0, 2:3] = colsum(dhr.astype(F32))
            go = mm(ctx_ref[...], dhr, 0, 0)

            @pl.when(step == 0)
            def _():
                go_ref[...] = go

            @pl.when(step > 0)
            def _():
                go_ref[...] += go

        state["dh"], state["dctx"], state["go"], state["back2"] = call(
            body,
            (steps,),
            [here(state["h"]), here(state["dy"]), in_hbm(state["ctx"]), w_out, g2]
            + [here(state["dc"]), here(state["dc_got"])],
            [rowD, rowD, rowW, in_vmem(), in_vmem(), rowD, rowD],
            [hbm((R, D), BF16), vmem((R, W), BF16), sds((W, D), F32), sds((steps, 3, D), F32)],
            [rowD, rowW, whole((W, D)), pl.BlockSpec((1, 3, D), lambda t: (t, 0, 0))],
            order=order,
            vmem=10,
        )

    def attn_back():
        def body(pr_ref, qkv_ref, dctx_ref, dqkv_ref, sum_ref):
            lane = lax.broadcasted_iota(jnp.int32, (SP, 128), 1)
            zero = jnp.zeros((SP, 128), BF16)
            for i in range(IB):
                rows = pl.ds(i * SP, SP)
                for j in range(pairs):
                    q = qkv_ref[rows, pl.ds(j * 128, 128)] * jnp.asarray(scale, BF16)
                    k = qkv_ref[rows, pl.ds(W + j * 128, 128)]
                    v = qkv_ref[rows, pl.ds(2 * W + j * 128, 128)]
                    dctx = dctx_ref[rows, pl.ds(j * 128, 128)]
                    dq = dk = dv = None
                    for s in range(2):
                        mine = (lane < 64) if s == 0 else (lane >= 64)
                        pr = pr_ref[i, 2 * j + s]
                        dc = jnp.where(mine, dctx, zero)
                        dv_h = mm(pr, dc)
                        dp = mm(v, dc, 1, 1)
                        p = pr.astype(F32)
                        pdp = p * dp
                        ds = (pdp - p * jnp.sum(pdp, axis=0, keepdims=True)).astype(BF16)
                        dk_h = mm(ds, jnp.where(mine, q, zero))
                        dq_h = mm(ds, jnp.where(mine, k, zero), 0, 0)
                        dq = dq_h if dq is None else dq + dq_h
                        dk = dk_h if dk is None else dk + dk_h
                        dv = dv_h if dv is None else dv + dv_h
                    dqkv_ref[rows, pl.ds(j * 128, 128)] = (dq * scale).astype(BF16)
                    dqkv_ref[rows, pl.ds(W + j * 128, 128)] = dk.astype(BF16)
                    dqkv_ref[rows, pl.ds(2 * W + j * 128, 128)] = dv.astype(BF16)
            sum_ref[0] = colsum(dqkv_ref[...].astype(F32))

        state["dqkv"], state["qkv_sums"] = call(
            body,
            (steps,),
            [in_hbm(state["pr"]), in_hbm(state["qkv"]), here(state["dctx"])],
            [pl.BlockSpec((IB, heads, SP, SP), lambda t: (t, 0, 0, 0)), row3, rowW],
            [vmem((R, 3 * W), BF16), sds((steps, 1, 3 * W), F32)],
            [row3, pl.BlockSpec((1, 1, 3 * W), lambda t: (t, 0, 0))],
            order=order,
            vmem=8,
        )

    def da():
        def body(d_ref, w_ref, o_ref):
            v = None
            for c in range(3):
                term = mm(d_ref[:, pl.ds(c * W, W)], w_ref[c], 1, 1)
                v = term if v is None else v + term
            o_ref[...] = v

        (state["da"],) = call(
            body,
            (steps,),
            [here(state["dqkv"]), wq],
            [row3, in_vmem()],
            [vmem((R, D), F32)],
            [rowD],
            order=order,
            vmem=6,
        )

    DQ, WH = DH // 2, W // 2

    def packed(v):
        return jnp.concatenate([v[:DQ], v[DQ:]], axis=1)

    def gqkv():
        def body(p_ref, p4_ref, a_ref, dqkv_ref, go_ref, k3_ref, s3_ref, k4_ref, s4_ref, at, tmp):
            step = pl.program_id(0)
            p = p_ref[0]
            p4 = p4_ref[0]

            @pl.when(step == 0)
            def _():
                at[...] = a_ref[...].T

            @pl.when(step < 3)
            def _():
                g = mm(at[...], dqkv_ref[...])
                tmp[0] = packed(g[:DH])
                tmp[1] = packed(g[DH:])

            @pl.when(step < 2)
            def _():
                k3_ref[...] = tmp[p]
                s3_ref[...] = tmp[1 - p]

            @pl.when(step == 2)
            def _():
                k4_ref[...] = tmp[p4]
                s4_ref[...] = tmp[1 - p4]

            @pl.when(step == 3)
            def _():
                k4_ref[...] = go_ref[pl.ds(pl.multiple_of(p4 * WH, 8), WH), :]
                s4_ref[...] = go_ref[pl.ds(pl.multiple_of((1 - p4) * WH, 8), WH), :]

        first_half = pl.BlockSpec((DQ, D), lambda t: (jnp.minimum(t, 1), 0))
        second_half = pl.BlockSpec((DQ, D), lambda t: (jnp.maximum(t - 2, 0), 0))
        k3, s3, k4, s4 = call(
            body,
            (4,),
            [first[chunks], first[chunks + 1], state["a"], here(state["dqkv"]), state["go"]],
            [smem(), smem(), in_vmem(), pl.BlockSpec((R, W), lambda t: (0, jnp.minimum(t, 2))), in_vmem()],
            [vmem((DH, D), F32)] * 4,
            [first_half, first_half, second_half, second_half],
            [pltpu.VMEM((D, R), BF16), pltpu.VMEM((2, DQ, D), F32)],
            order=order,
            vmem=10,
        )

        def finish3(mine, got, order):
            def body(p_ref, m_ref, g_ref, *rest):
                o_ref = rest[-1]
                own = pl.program_id(0) == p_ref[0]

                def write(ref):
                    for c in range(2):
                        for b in range(2):
                            o_ref[c, pl.ds(b * DQ, DQ), :] = ref[pl.ds(c * DQ, DQ), pl.ds(b * W, W)]

                @pl.when(own)
                def _():
                    write(m_ref)

                @pl.when(jnp.logical_not(own))
                def _():
                    write(g_ref)

            ins, specs, aliases = [first[chunks], mine, got], [smem(), in_vmem(), in_vmem()], {}
            if "gqkv" in state:
                aliases = {3: 0}
                ins += [in_hbm(state["gqkv"])]
                specs += [anywhere()]
            (state["gqkv"],) = call(
                body, (2,), ins, specs, [hbm((3, D, W), F32)],
                [pl.BlockSpec((2, DH, W), lambda t: (0, t, 0))], aliases=aliases, order=order, vmem=10,
            )

        def finish4(mine, got, order):
            def body(p_ref, m_ref, g_ref, *rest):
                o_ref, go_ref = rest[-2:]
                own = pl.program_id(0) == p_ref[0]

                def write(ref):
                    for b in range(2):
                        o_ref[0, pl.ds(b * DQ, DQ), :] = ref[pl.ds(0, DQ), pl.ds(b * W, W)]
                    go_ref[...] = ref[pl.ds(DQ, WH), :]

                @pl.when(own)
                def _():
                    write(m_ref)

                @pl.when(jnp.logical_not(own))
                def _():
                    write(g_ref)

            ins, specs, aliases = [first[chunks + 1], mine, got], [smem(), in_vmem(), in_vmem()], {}
            if "gqkv" in state:
                aliases = {3: 0}
                ins += [in_hbm(state["gqkv"])]
                specs += [anywhere()]
            state["gqkv"], state["grad_out"] = call(
                body, (2,), ins, specs, [hbm((3, D, W), F32), hbm((W, D), F32)],
                [pl.BlockSpec((1, DH, W), lambda t: (2, t, 0)), pl.BlockSpec((WH, D), lambda t: (t, 0))],
                aliases=aliases, order=order, vmem=10,
            )

        def start():
            send3, send4 = release([s3, s4], vmem)
            pieces[chunks] = Piece(links, sides, plan["dims"][chunks], k3, send3, finish3)
            pieces[chunks + 1] = Piece(links, sides, plan["dims"][chunks + 1], k4, send4, finish4)

        state["qkv_send"] = start

    def gather_rows(ys, o_ref):
        @pl.when(pl.program_id(0) == steps - 1)
        def _():
            for k in range(D // 128):
                v = ys[k, pl.ds(0, seq * items), :].reshape(seq, items, 128)
                o_ref[:, :, pl.ds(k * 128, 128)] = v.astype(BF16)

    def put_rows(ys, v):
        step = pl.program_id(0)
        for j in range(steps):

            @pl.when(step == j)
            def _(j=j):
                for i in range(IB):
                    for k in range(D // 128):
                        ys[k, pl.ds(j * IB + i, SP, stride=items), :] = v[
                            i * SP : (i + 1) * SP, k * 128 : (k + 1) * 128
                        ]

    def back1():
        def body(x_ref, dh_ref, g_ref, e0_ref, e1_ref, o_ref, sum_ref, ys):
            e = e0_ref[...] + e1_ref[...]
            n, inverse = normed(x_ref[...].astype(F32))
            dx = dh_ref[...].astype(F32) + norm_back(e, n, inverse, g_ref[...])
            put_rows(ys, dx)
            sum_ref[0, 0:1] = colsum(e * n)
            sum_ref[0, 1:2] = colsum(e)
            gather_rows(ys, o_ref)

        state["grad_tokens"], state["back1"] = call(
            body,
            (steps,),
            [in_hbm(state["x_kept"]), in_hbm(state["dh"]), g1, here(state["da"]), here(state["da_got"])],
            [rowD, rowD, in_vmem(), rowD, rowD],
            [hbm((seq, items, D), BF16), sds((steps, 2, D), F32)],
            [whole((seq, items, D)), pl.BlockSpec((1, 2, D), lambda t: (t, 0, 0))],
            [pltpu.VMEM((D // 128, SP * items, 128), F32)],
            order=order,
            vmem=17,
        )

    def out():
        def body(cnt_ref, h_ref, p_ref, r_ref, b_ref, o_ref, ys):
            step = pl.program_id(0)
            v = h_ref[...].astype(F32) + (p_ref[...] + r_ref[...]) + b_ref[...]
            item = step * IB + lax.broadcasted_iota(jnp.int32, (BR, D), 0) // SP
            put_rows(ys, jnp.where(item < cnt_ref[0], v, 0.0))
            gather_rows(ys, o_ref)

        (state["output"],) = call(
            body,
            (steps,),
            [item_counts, here(state["h"]), here(state["y"]), here(state["y_got"]), down_b],
            [smem(), rowD, rowD, rowD, in_vmem()],
            [hbm((seq, items, D), BF16)],
            [whole((seq, items, D))],
            [pltpu.VMEM((D // 128, SP * items, 128), F32)],
            order=order,
            vmem=17,
        )

    SR = 16

    def gather():
        def body(q_ref, b2_ref, dy_ref, b1_ref, *rest):
            ups, o_ref = rest[:-1], rest[-1]
            o_ref[...] = jnp.zeros((SR, D), F32)
            qs = jnp.sum(q_ref[...], axis=0)
            o_ref[0:1, pl.ds(0, W)] = qs[:, :W]
            o_ref[0:1, pl.ds(W, W)] = qs[:, 2 * W :]
            o_ref[1:4, :] = jnp.sum(b2_ref[...], axis=0)
            for up, at, hu in zip(ups, starts, sizes):
                for side in range(2):
                    o_ref[4 + side : 5 + side, pl.ds(at, hu)] = up[:, pl.ds(side * hu, hu)]
            o_ref[6:7, :] = dy_ref[...]
            o_ref[7:9, :] = jnp.sum(b1_ref[...], axis=0)

        ins = [state["qkv_sums"], state["back2"], state["dy_sum"], state["back1"]] + up_sums
        state["small"] = call(
            body, (), ins, [in_vmem()] * len(ins), [sds((SR, D), F32)], [in_vmem()], order=order, vmem=8
        )[0]
        state["small_dims"] = [("x", "y"), ("y", "x"), ("a", "a"), ("b", "b")] + [(e, e) for e in links.extra]
        state["small_got"] = links.swap(state["small"], state["small_dims"].pop(0))

    def small():
        if state["small_dims"]:
            state["small"] = add(state["small"], state["small_got"], order)
            state["small_got"] = links.swap(state["small"], state["small_dims"].pop(0))
            return

        def body(a_ref, b_ref, qb_ref, ob_ref, ub_ref, db_ref, gg_ref, gb_ref):
            s = a_ref[...] + b_ref[...]
            qb_ref[0:1, :] = s[0:1, :W]
            qb_ref[1:2, :] = s[0:1, W:]
            gg_ref[1:2, :] = s[1:2]
            gb_ref[1:2, :] = s[2:3]
            ob_ref[...] = s[3]
            ub_ref[pl.ds(0, D)] = s[4]
            ub_ref[pl.ds(D, D)] = s[5]
            db_ref[...] = s[6]
            gg_ref[0:1, :] = s[7:8]
            gb_ref[0:1, :] = s[8:9]

        shapes = [(2, W), (D,), (FL,), (D,), (2, D), (2, D)]
        state["small_outs"] = call(
            body, (), [state["small"], state["small_got"]], [in_vmem()] * 2,
            [sds(v, F32) for v in shapes], [in_vmem()] * len(shapes), order=order, vmem=8,
        )

    jobs = {
        "dc": dc, "y": y, "back2": back2, "attn": attn_back, "gqkv": gqkv, "da": da, "back1": back1, "out": out,
        "gather": gather, "small": small, "dc_send": dc_send, "da_send": da_send, "y_send": y_send,
        "qkv_send": lambda: state["qkv_send"](),
    }
    for job in plan["order"]:
        if job in jobs:
            jobs[job]()
        elif job.startswith("F"):
            ffn(int(job[1:]))
        else:
            pieces[int(job)].step(order)
    for piece in pieces.values():
        while piece.at < len(piece.stages):
            piece.step(order)
    while "small_outs" not in state:
        small()
    qb, ob, ub, db, gg, gb = state["small_outs"]
    return (
        jnp.transpose(state["output"], by_token),
        jnp.transpose(state["grad_tokens"], by_token),
        jnp.transpose(state["gqkv"], (1, 0, 2)),
        qb,
        state["grad_out"],
        ob,
        state["gu"],
        ub,
        state["gd"],
        db,
        gg,
        gb,
    )


PLAN = {
    "units": (1, 1, 2, 2),
    "dims": (("yxab", "xyab"), ("yxab", "xyab"), ("ayxb", "axyb"), ("yxab", "xyab"), ("yxab", "xyab"), ("yxab", "xyab")),
    "order": (
        "F0", "F1", "F2", "F3", "0", "dc", "1", "dc_send", "back2", "attn", "3", "1", "0", "gqkv", "qkv_send", "3",
        "1", "2", "3", "5", "1", "0", "da", "4", "1", "3", "2", "y", "0", "y_send", "4", "5", "2", "3", "da_send",
        "out", "3", "4", "back1", "2", "5", "1", "4", "2", "gather", "0", "5", "4", "1", "0", "small", "5", "3",
        "2", "small", "5", "0", "4", "5", "small", "small", "2", "4",
    ),
}


def solution(mesh):
    links = Links(mesh.shape["dp"], mesh.shape["tensor"])

    def layer(*arrays):
        return on_device(links, PLAN, *arrays)

    return jax.shard_map(
        layer,
        mesh=mesh,
        in_specs=(
            P("dp", None, None),
            P("dp", None, None),
            P("dp"),
            P("dp"),
            P(None, None, "tensor"),
            P(None, "tensor"),
            P("tensor", None),
            P(),
            P(None, "tensor"),
            P("tensor"),
            P("tensor", None),
            P(),
            P(),
            P(),
        ),
        out_specs=(
            P("dp", None, None),
            P("dp", None, None),
            P(None, None, "tensor"),
            P(None, "tensor"),
            P("tensor", None),
            P(),
            P(None, "tensor"),
            P("tensor"),
            P("tensor", None),
            P(),
            P(),
            P(),
        ),
        check_vma=False,
    )
```

profile of v0, /device:TPU:0, one launch (start us, length us, event | category | flops | bytes accessed | tf_op | source)
XLA Modules:
  0.0 273.7 jit_solution(3319651279696633588)
XLA Ops:
  6.7 6.4 %shard_map.230 = (f32[768,768]{1,0:T(8,128)S(1)}, bf16[1536,768]{1,0:T(8,128)(2,1)}, bf16[1536,1152]{1,0:T(8,128)(2,1)}, bf16[8,6,192,192]{3,2,1,0:T(8,128)(2,1)...) custom-call(s32[8]{0:T(128)S(1)} %copy-done.7, ...), custom_call_target="tpu_custom_call" | custom-call | flops 1024 | bytes 1024 | tf_op jit(solution)/shard_map/pallas_call | solution.py:53
  13.5 6.4 %shard_map.231 = (f32[768,768]{1,0:T(8,128)S(1)}, bf16[1536,768]{1,0:T(8,128)(2,1)}, bf16[1536,1152]{1,0:T(8,128)(2,1)}, bf16[8,6,192,192]{3,2,1,0:T(8,128)(2,1)...) custom-call(s32[8]{0:T(128)S(1)} %copy-done.7, ...), custom_call_target="tpu_custom_call", output_to_operand_aliasing={{1}: (7, {}), {2}: (8, {}), {3}: (9, {}), {4}: (10, {}), {5... | custom-call | flops 1024 | bytes 1024 | tf_op jit(solution)/shard_map/pallas_call | solution.py:53
  19.9 10.8 %collective-permute-start = (f32[768,768]{1,0:T(8,128)S(1)}, f32[768,768]{1,0:T(8,128)S(1)}, u32[]{:S(2)}, u32[]{:S(2)}) collective-permute-start(f32[768,768]{1,0:T(8,128)S(1)} %get-tuple-element.219.refs_1_), channel_id=1, source_target_pairs={{0,1},{1,0},{2,3},{3,2},{4,5},{5,4},{6,7},{7,6},{8,9},{9,8},{10,11... | collective-permute-start | bytes 7077896 | tf_op jit(solution)/shard_map/ppermute | solution.py:239
  46.1 5.5 %shard_map.237 = (f32[512,768]{1,0:T(8,128)S(1)}, f32[512,768]{1,0:T(8,128)S(1)}, f32[1,512]{1,0:T(1,128)S(1)}, bf16[1536,512]{1,0:T(8,128)(2,1)S(1)}, bf16[1536,512]{1,0:T(8,128)(2,1)S(1)}, /*index=5*/f32[8,128]{1,0:T(8,128)}) custom-call(s32[1]{0:T(128)} %bitcast.10.refs_11_.refs_0_, bf16[1536,768]{1,0:T(8,128)(2,1)S(1)} %get-tuple-element.228.refs_1_, ...), custom_call_target="tpu_custom_call" | custom-call | flops 1024 | bytes 1024 | tf_op jit(solution)/shard_map/pallas_call | solution.py:53
  51.6 5.9 %shard_map.238 = (f32[512,768]{1,0:T(8,128)S(1)}, f32[512,768]{1,0:T(8,128)S(1)}, f32[1,512]{1,0:T(1,128)S(1)}, bf16[1536,512]{1,0:T(8,128)(2,1)S(1)}, bf16[1536,512]{1,0:T(8,128)(2,1)S(1)}, /*index=5*/f32[8,128]{1,0:T(8,128)}) custom-call(s32[1]{0:T(128)} %bitcast.4.refs_5_.refs_0_.refs_1_, bf16[1536,768]{1,0:T(8,128)(2,1)S(1)} %get-tuple-element.228.refs_1_, ...), custom_call_target="tpu_custom_call" | custom-call | flops 1024 | bytes 1024 | tf_op jit(solution)/shard_map/pallas_call | solution.py:53
  57.6 4.4 %shard_map.240 = (f32[1536,768]{1,0:T(8,128)S(1)}, f32[8,128]{1,0:T(8,128)}) custom-call(bf16[1536,256]{1,0:T(8,128)(2,1)S(1)} %get-tuple-element.243.refs_0_, bf16[1536,256]{1,0:T(8,128)(2,1)S(1)} %get-tuple-element.244.refs_1_, bf16[1536,512]{1,0:T(8,128)(2,1)S(1)} %get-tuple-element.245.refs_2_, bf16[1536,512]{1,0:T(8,128)(2,1)S(1)} %get-tuple-element.246.refs_3_, ...), custom_call_target="tpu_custom_call" | custom-call | flops 1024 | bytes 1024 | tf_op jit(solution)/shard_map/pallas_call | solution.py:53
  70.1 8.7 %shard_map.243 = (bf16[1536,768]{1,0:T(8,128)(2,1)}, bf16[1536,384]{1,0:T(8,128)(2,1)S(1)}, f32[384,768]{1,0:T(8,128)S(1)}, f32[4,3,768]{2,1,0:T(4,128)S(1)}, f32[8,128]{1,0:T(8,128)}) custom-call(bf16[1536,768]{1,0:T(8,128)(2,1)S(1)} %get-tuple-element.227.refs_0_.refs_1_, bf16[1536,768]{1,0:T(8,128)(2,1)S(1)} %get-tuple-element.230.refs_3_.refs_1_, ...), custom_call_target="tpu_custom_call" | custom-call | flops 1024 | bytes 1024 | tf_op jit(solution)/shard_map/pallas_call | solution.py:53
  78.8 12.1 %shard_map.244 = (bf16[1536,1152]{1,0:T(8,128)(2,1)S(1)}, f32[4,1,1152]{2,1,0:T(1,128)S(1)}, f32[8,128]{1,0:T(8,128)}) custom-call(bf16[8,6,192,192]{3,2,1,0:T(8,128)(2,1)} %get-tuple-element.256.refs_0_, bf16[1536,1152]{1,0:T(8,128)(2,1)} %get-tuple-element.257.refs_1_, bf16[1536,384]{1,0:T(8,128)(2,1)S(1)} %get-tuple-element.263.refs_2_, ...), custom_call_target="tpu_custom_call" | custom-call | flops 1024 | bytes 1024 | tf_op jit(solution)/shard_map/pallas_call | solution.py:53
  93.5 5.6 %shard_map.248 = (f32[384,768]{1,0:T(8,128)S(1)}, f32[384,768]{1,0:T(8,128)S(1)}, f32[384,768]{1,0:T(8,128)S(1)}, f32[384,768]{1,0:T(8,128)S(1)}, f32[8,128]{1,0:T(8,128)}) custom-call(s32[1]{0:T(128)} %bitcast.4.refs_5_.refs_0_.refs_1_, s32[1]{0:T(128)} %bitcast.4.refs_5_.refs_0_.refs_1_, bf16[1536,768]{1,0:T(8,128)(2,1)S(1)} %copy-done.3, ...), custom_call_target="tpu_custom_call" | custom-call | flops 1024 | bytes 1024 | tf_op jit(solution)/shard_map/pallas_call | solution.py:53
  113.1 7.7 %collective-permute-done.12.refs_1_ = f32[128,768]{1,0:T(8,128)S(1)} collective-permute-done((f32[128,768]{1,0:T(8,128)S(1)}, f32[128,768]{1,0:T(8,128)S(1)}, u32[]{:S(2)}, u32[]{:S(2)}) %collective-permute-start.12) | collective-permute-done | bytes 393248 | tf_op jit(solution)/shard_map/ppermute | solution.py:112
  120.9 5.7 %collective-permute-start.13 = (f32[128,768]{1,0:T(8,128)S(1)}, f32[128,768]{1,0:T(8,128)S(1)}, u32[]{:S(2)}, u32[]{:S(2)}) collective-permute-start(f32[128,768]{1,0:T(8,128)S(1)} %get-tuple-element.289.refs_0_), channel_id=1, source_target_pairs={{0,16},{1,17},{2,18},{3,19},{4,20},{5,21},{6,22},{7,23},{8,24},{9,... | collective-permute-start | bytes 1179656 | tf_op jit(solution)/shard_map/ppermute | solution.py:112
  128.9 4.4 %shard_map.257 = (f32[1536,768]{1,0:T(8,128)S(1)}, f32[8,128]{1,0:T(8,128)}) custom-call(bf16[1536,1152]{1,0:T(8,128)(2,1)S(1)} %get-tuple-element.272.refs_3_.refs_0_, bf16[3,768,384]{2,1,0:T(8,128)(2,1)S(1)} %bitcast.24, f32[8,128]{1,0:T(8,128)} %get-tuple-element.301.refs_2_), custom_call_target="tpu_custom_call" | custom-call | flops 1024 | bytes 1024 | tf_op jit(solution)/shard_map/pallas_call | solution.py:53
  137.5 3.8 %collective-permute-start.19 = (f32[64,768]{1,0:T(8,128)S(1)}, f32[64,768]{1,0:T(8,128)S(1)}, u32[]{:S(2)}, u32[]{:S(2)}) collective-permute-start(f32[64,768]{1,0:T(8,128)S(1)} %get-tuple-element.308.refs_0_), channel_id=1, source_target_pairs={{0,16},{1,17},{2,18},{3,19},{4,20},{5,21},{6,22},{7,23},{8,24},{9,... | collective-permute-start | bytes 589832 | tf_op jit(solution)/shard_map/ppermute | solution.py:112
  145.0 4.5 %shard_map.262 = (f32[1536,768]{1,0:T(8,128)S(1)}, f32[8,128]{1,0:T(8,128)}) custom-call(bf16[1536,256]{1,0:T(8,128)(2,1)S(1)} %get-tuple-element.232.refs_0_, bf16[1536,256]{1,0:T(8,128)(2,1)S(1)} %get-tuple-element.234.refs_1_, bf16[1536,512]{1,0:T(8,128)(2,1)S(1)} %get-tuple-element.236.refs_2_, bf16[1536,512]{1,0:T(8,128)(2,1)S(1)} %get-tuple-element.238.refs_3_, ...), custom_call_target="tpu_custom_call" | custom-call | flops 1024 | bytes 1024 | tf_op jit(solution)/shard_map/pallas_call | solution.py:53
  149.9 4.1 %collective-permute-done.22.refs_1_ = f32[128,768]{1,0:T(8,128)S(1)} collective-permute-done((f32[128,768]{1,0:T(8,128)S(1)}, f32[128,768]{1,0:T(8,128)S(1)}, u32[]{:S(2)}, u32[]{:S(2)}) %collective-permute-start.22) | collective-permute-done | bytes 393248 | tf_op jit(solution)/shard_map/ppermute | solution.py:112
  162.1 4.8 %shard_map.270 = (bf16[185,8,768]{2,1,0:T(8,128)(2,1)}, f32[8,128]{1,0:T(8,128)}) custom-call(s32[1]{0:T(128)S(6)} %copy.66.refs_0_, bf16[1536,768]{1,0:T(8,128)(2,1)S(1)} %get-tuple-element.227.refs_0_.refs_1_, f32[1536,768]{1,0:T(8,128)S(1)} %get-tuple-element.311.refs_2_, f32[1536,768]{1,0:T(8,128)S(1)} %collective-permute-done.20.refs_3_, ...), custom_call_target="tpu_custom_call" | custom-call | flops 1024 | bytes 1024 | tf_op jit(solution)/shard_map/pallas_call | solution.py:53
  174.8 8.7 %shard_map.273 = (bf16[185,8,768]{2,1,0:T(8,128)(2,1)}, f32[4,2,768]{2,1,0:T(2,128)S(1)}, f32[8,128]{1,0:T(8,128)}) custom-call(bf16[1536,768]{1,0:T(8,128)(2,1)} %get-tuple-element.327.refs_0_, bf16[1536,768]{1,0:T(8,128)(2,1)} %get-tuple-element.328.refs_1_, f32[1,768]{1,0:T(1,128)S(1)} %get-tuple-element.416.refs_4_.refs_2_, ...), custom_call_target="tpu_custom_call" | custom-call | flops 1024 | bytes 1024 | tf_op jit(solution)/shard_map/pallas_call | solution.py:53
  187.9 10.4 %collective-permute-done.28.refs_1_ = f32[96,768]{1,0:T(8,128)S(1)} collective-permute-done((f32[96,768]{1,0:T(8,128)S(1)}, f32[96,768]{1,0:T(8,128)S(1)}, u32[]{:S(2)}, u32[]{:S(2)}) %collective-permute-start.28) | collective-permute-done | bytes 294944 | tf_op jit(solution)/shard_map/ppermute | solution.py:112
  200.6 7.5 %collective-permute-done.34.refs_2_ = f32[64,768]{1,0:T(8,128)S(1)} collective-permute-done((f32[64,768]{1,0:T(8,128)S(1)}, f32[64,768]{1,0:T(8,128)S(1)}, u32[]{:S(2)}, u32[]{:S(2)}) %collective-permute-start.34) | collective-permute-done | bytes 196640 | tf_op jit(solution)/shard_map/ppermute | solution.py:112
  213.5 6.7 %collective-permute-done.37.refs_2_ = f32[128,768]{1,0:T(8,128)S(1)} collective-permute-done((f32[128,768]{1,0:T(8,128)S(1)}, f32[128,768]{1,0:T(8,128)S(1)}, u32[]{:S(2)}, u32[]{:S(2)}) %collective-permute-start.37) | collective-permute-done | bytes 393248 | tf_op jit(solution)/shard_map/ppermute | solution.py:112
  231.7 9.3 %collective-permute-done.44.refs_1_ = f32[16,768]{1,0:T(8,128)S(1)} collective-permute-done((f32[16,768]{1,0:T(8,128)S(1)}, f32[16,768]{1,0:T(8,128)S(1)}, u32[]{:S(2)}, u32[]{:S(2)}) %collective-permute-start.44) | collective-permute-done | bytes 49184 | tf_op jit(solution)/shard_map/ppermute | solution.py:112
  243.6 8.6 %collective-permute-done.36.refs_2_ = f32[192,768]{1,0:T(8,128)S(1)} collective-permute-done((f32[192,768]{1,0:T(8,128)S(1)}, f32[192,768]{1,0:T(8,128)S(1)}, u32[]{:S(2)}, u32[]{:S(2)}) %collective-permute-start.36) | collective-permute-done | bytes 589856 | tf_op jit(solution)/shard_map/ppermute | solution.py:112
  252.5 5.6 %collective-permute-done.47.refs_2_ = f32[384,768]{1,0:T(8,128)S(1)} collective-permute-done((f32[384,768]{1,0:T(8,128)S(1)}, f32[384,768]{1,0:T(8,128)S(1)}, u32[]{:S(2)}, u32[]{:S(2)}) %collective-permute-start.47) | collective-permute-done | bytes 1179680 | tf_op jit(solution)/shard_map/ppermute | solution.py:112
  259.5 3.9 %collective-permute-done.49.refs_1_ = f32[16,768]{1,0:T(8,128)S(1)} collective-permute-done((f32[16,768]{1,0:T(8,128)S(1)}, f32[16,768]{1,0:T(8,128)S(1)}, u32[]{:S(2)}, u32[]{:S(2)}) %collective-permute-start.49) | collective-permute-done | bytes 49184 | tf_op jit(solution)/shard_map/ppermute | solution.py:112
  (177 shorter events, 109.9 us)
Async XLA Ops:
  13.0 17.8 %collective-permute-start.1 = (f32[768,768]{1,0:T(8,128)S(1)}, f32[768,768]{1,0:T(8,128)S(1)}, u32[]{:S(2)}, u32[]{:S(2)}) collective-permute-start(f32[768,768]{1,0:T(8,128)S(1)} %get-tuple-element.220.refs_1_), channel_id=1, source_target_pairs={{0,1},{1,0},{2,3},{3,2},{4,5},{5,4},{6,7},{7,6},{8,9},{9,8},{10,11... | collective-permute-start | bytes 7077896 | tf_op jit(solution)/shard_map/ppermute | solution.py:239
  40.5 17.0 %collective-permute-start.4 = (f32[256,768]{1,0:T(8,128)S(1)}, f32[256,768]{1,0:T(8,128)S(1)}, u32[]{:S(2)}, u32[]{:S(2)}) collective-permute-start(f32[256,768]{1,0:T(8,128)S(1)} %get-tuple-element.248), channel_id=1, source_target_pairs={{0,4},{1,3},{2,6},{3,1},{4,0},{5,7},{6,2},{7,5},{8,12},{9,11},{10,... | collective-permute-start | bytes 2359304 | tf_op jit(solution)/shard_map/ppermute | solution.py:112
  62.4 28.8 %collective-permute-start.6 = (f32[512,768]{1,0:T(8,128)S(1)}, f32[512,768]{1,0:T(8,128)S(1)}, u32[]{:S(2)}, u32[]{:S(2)}) collective-permute-start(f32[512,768]{1,0:T(8,128)S(1)} %get-tuple-element.255), channel_id=1, source_target_pairs={{0,4},{1,3},{2,6},{3,1},{4,0},{5,7},{6,2},{7,5},{8,12},{9,11},{10,... | collective-permute-start | bytes 4718600 | tf_op jit(solution)/shard_map/ppermute | solution.py:112
  64.3 44.5 %collective-permute-start.2 = (f32[512,768]{1,0:T(8,128)S(1)}, f32[512,768]{1,0:T(8,128)S(1)}, u32[]{:S(2)}, u32[]{:S(2)}) collective-permute-start(f32[512,768]{1,0:T(8,128)S(1)} %get-tuple-element.240), channel_id=1, source_target_pairs={{0,8},{1,9},{2,10},{3,11},{4,12},{5,13},{6,14},{7,15},{8,0},{9,1},... | collective-permute-start | bytes 4718600 | tf_op jit(solution)/shard_map/ppermute | solution.py:112
  65.9 27.5 %collective-permute-start.5 = (f32[128,768]{1,0:T(8,128)S(1)}, f32[128,768]{1,0:T(8,128)S(1)}, u32[]{:S(2)}, u32[]{:S(2)}) collective-permute-start(f32[128,768]{1,0:T(8,128)S(1)} %get-tuple-element.253), channel_id=1, source_target_pairs={{0,2},{1,5},{2,0},{3,7},{4,6},{5,1},{6,4},{7,3},{8,10},{9,13},{10,... | collective-permute-start | bytes 1179656 | tf_op jit(solution)/shard_map/ppermute | solution.py:112
  67.4 26.0 %collective-permute-start.10 = (f32[128,768]{1,0:T(8,128)S(1)}, f32[128,768]{1,0:T(8,128)S(1)}, u32[]{:S(2)}, u32[]{:S(2)}) collective-permute-start(f32[128,768]{1,0:T(8,128)S(1)} %get-tuple-element.275), channel_id=1, source_target_pairs={{0,2},{1,5},{2,0},{3,7},{4,6},{5,1},{6,4},{7,3},{8,10},{9,13},{10,... | collective-permute-start | bytes 1179656 | tf_op jit(solution)/shard_map/ppermute | solution.py:112
  99.2 21.7 %collective-permute-start.15 = (f32[384,768]{1,0:T(8,128)S(1)}, f32[384,768]{1,0:T(8,128)S(1)}, u32[]{:S(2)}, u32[]{:S(2)}) collective-permute-start(f32[384,768]{1,0:T(8,128)S(1)} %get-tuple-element.292), channel_id=1, source_target_pairs={{0,4},{1,3},{2,6},{3,1},{4,0},{5,7},{6,2},{7,5},{8,12},{9,11},{10,... | collective-permute-start | bytes 3538952 | tf_op jit(solution)/shard_map/ppermute | solution.py:112
  100.8 32.6 %collective-permute-start.17 = (f32[384,768]{1,0:T(8,128)S(1)}, f32[384,768]{1,0:T(8,128)S(1)}, u32[]{:S(2)}, u32[]{:S(2)}) collective-permute-start(f32[384,768]{1,0:T(8,128)S(1)} %get-tuple-element.297), channel_id=1, source_target_pairs={{0,4},{1,3},{2,6},{3,1},{4,0},{5,7},{6,2},{7,5},{8,12},{9,11},{10,... | collective-permute-start | bytes 3538952 | tf_op jit(solution)/shard_map/ppermute | solution.py:112
  109.0 34.2 %collective-permute-start.11 = (f32[256,768]{1,0:T(8,128)S(1)}, f32[256,768]{1,0:T(8,128)S(1)}, u32[]{:S(2)}, u32[]{:S(2)}) collective-permute-start(f32[256,768]{1,0:T(8,128)S(1)} %get-tuple-element.285), channel_id=1, source_target_pairs={{0,4},{1,3},{2,6},{3,1},{4,0},{5,7},{6,2},{7,5},{8,12},{9,11},{10,... | collective-permute-start | bytes 2359304 | tf_op jit(solution)/shard_map/ppermute | solution.py:112
  120.9 22.3 %collective-permute-start.13 = (f32[128,768]{1,0:T(8,128)S(1)}, f32[128,768]{1,0:T(8,128)S(1)}, u32[]{:S(2)}, u32[]{:S(2)}) collective-permute-start(f32[128,768]{1,0:T(8,128)S(1)} %get-tuple-element.289.refs_0_), channel_id=1, source_target_pairs={{0,16},{1,17},{2,18},{3,19},{4,20},{5,21},{6,22},{7,23},{8,24},{9,... | collective-permute-start | bytes 1179656 | tf_op jit(solution)/shard_map/ppermute | solution.py:112
  133.5 16.2 %collective-permute-start.24 = (f32[192,768]{1,0:T(8,128)S(1)}, f32[192,768]{1,0:T(8,128)S(1)}, u32[]{:S(2)}, u32[]{:S(2)}) collective-permute-start(f32[192,768]{1,0:T(8,128)S(1)} %get-tuple-element.319), channel_id=1, source_target_pairs={{0,2},{1,5},{2,0},{3,7},{4,6},{5,1},{6,4},{7,3},{8,10},{9,13},{10,... | collective-permute-start | bytes 1769480 | tf_op jit(solution)/shard_map/ppermute | solution.py:112
  154.2 18.1 %collective-permute-start.25 = (f32[1536,768]{1,0:T(8,128)S(1)}, f32[1536,768]{1,0:T(8,128)S(1)}, u32[]{:S(2)}, u32[]{:S(2)}) collective-permute-start(f32[1536,768]{1,0:T(8,128)S(1)} %get-tuple-element.329.refs_3_), channel_id=1, source_target_pairs={{0,1},{1,0},{2,3},{3,2},{4,5},{5,4},{6,7},{7,6},{8,9},{9,8},{10,11... | collective-permute-start | bytes 14155784 | tf_op jit(solution)/shard_map/ppermute | solution.py:239
  157.6 25.8 %collective-permute-start.31 = (f32[128,768]{1,0:T(8,128)S(1)}, f32[128,768]{1,0:T(8,128)S(1)}, u32[]{:S(2)}, u32[]{:S(2)}) collective-permute-start(f32[128,768]{1,0:T(8,128)S(1)} %get-tuple-element.341.refs_0_), channel_id=1, source_target_pairs={{0,16},{1,17},{2,18},{3,19},{4,20},{5,21},{6,22},{7,23},{8,24},{9,... | collective-permute-start | bytes 1179656 | tf_op jit(solution)/shard_map/ppermute | solution.py:112
  160.9 26.8 %collective-permute-start.29 = (f32[128,768]{1,0:T(8,128)S(1)}, f32[128,768]{1,0:T(8,128)S(1)}, u32[]{:S(2)}, u32[]{:S(2)}) collective-permute-start(f32[128,768]{1,0:T(8,128)S(1)} %get-tuple-element.338.refs_1_), channel_id=1, source_target_pairs={{0,2},{1,5},{2,0},{3,7},{4,6},{5,1},{6,4},{7,3},{8,10},{9,13},{10,... | collective-permute-start | bytes 1179656 | tf_op jit(solution)/shard_map/ppermute | solution.py:112
  167.0 61.3 %collective-permute-start.40 = (f32[512,768]{1,0:T(8,128)S(1)}, f32[512,768]{1,0:T(8,128)S(1)}, u32[]{:S(2)}, u32[]{:S(2)}) collective-permute-start(f32[512,768]{1,0:T(8,128)S(1)} %get-tuple-element.369.refs_1_), channel_id=1, source_target_pairs={{0,4},{1,3},{2,6},{3,1},{4,0},{5,7},{6,2},{7,5},{8,12},{9,11},{10,... | collective-permute-start | bytes 4718600 | tf_op jit(solution)/shard_map/ppermute | solution.py:112
  172.2 26.1 %collective-permute-start.28 = (f32[96,768]{1,0:T(8,128)S(1)}, f32[96,768]{1,0:T(8,128)S(1)}, u32[]{:S(2)}, u32[]{:S(2)}) collective-permute-start(f32[96,768]{1,0:T(8,128)S(1)} %get-tuple-element.337.refs_0_), channel_id=1, source_target_pairs={{0,16},{1,17},{2,18},{3,19},{4,20},{5,21},{6,22},{7,23},{8,24},{9,... | collective-permute-start | bytes 884744 | tf_op jit(solution)/shard_map/ppermute | solution.py:112
  187.8 23.7 %collective-permute-start.38 = (f32[256,768]{1,0:T(8,128)S(1)}, f32[256,768]{1,0:T(8,128)S(1)}, u32[]{:S(2)}, u32[]{:S(2)}) collective-permute-start(f32[256,768]{1,0:T(8,128)S(1)} %get-tuple-element.365.refs_1_), channel_id=1, source_target_pairs={{0,4},{1,3},{2,6},{3,1},{4,0},{5,7},{6,2},{7,5},{8,12},{9,11},{10,... | collective-permute-start | bytes 2359304 | tf_op jit(solution)/shard_map/ppermute | solution.py:112
  187.8 21.2 %collective-permute-start.33 = (f32[96,768]{1,0:T(8,128)S(1)}, f32[96,768]{1,0:T(8,128)S(1)}, u32[]{:S(2)}, u32[]{:S(2)}) collective-permute-start(f32[96,768]{1,0:T(8,128)S(1)} %get-tuple-element.347.refs_0_), channel_id=1, source_target_pairs={{0,16},{1,17},{2,18},{3,19},{4,20},{5,21},{6,22},{7,23},{8,24},{9,... | collective-permute-start | bytes 884744 | tf_op jit(solution)/shard_map/ppermute | solution.py:112
  209.0 21.6 %collective-permute-start.45 = (f32[256,768]{1,0:T(8,128)S(1)}, f32[256,768]{1,0:T(8,128)S(1)}, u32[]{:S(2)}, u32[]{:S(2)}) collective-permute-start(f32[256,768]{1,0:T(8,128)S(1)} %get-tuple-element.381.refs_1_), channel_id=1, source_target_pairs={{0,4},{1,3},{2,6},{3,1},{4,0},{5,7},{6,2},{7,5},{8,12},{9,11},{10,... | collective-permute-start | bytes 2359304 | tf_op jit(solution)/shard_map/ppermute | solution.py:112
  220.2 21.6 %collective-permute-start.39 = (f32[256,768]{1,0:T(8,128)S(1)}, f32[256,768]{1,0:T(8,128)S(1)}, u32[]{:S(2)}, u32[]{:S(2)}) collective-permute-start(f32[256,768]{1,0:T(8,128)S(1)} %get-tuple-element.368.refs_1_), channel_id=1, source_target_pairs={{0,4},{1,3},{2,6},{3,1},{4,0},{5,7},{6,2},{7,5},{8,12},{9,11},{10,... | collective-permute-start | bytes 2359304 | tf_op jit(solution)/shard_map/ppermute | solution.py:112
  227.2 25.0 %collective-permute-start.36 = (f32[192,768]{1,0:T(8,128)S(1)}, f32[192,768]{1,0:T(8,128)S(1)}, u32[]{:S(2)}, u32[]{:S(2)}) collective-permute-start(f32[192,768]{1,0:T(8,128)S(1)} %get-tuple-element.363.refs_1_), channel_id=1, source_target_pairs={{0,2},{1,5},{2,0},{3,7},{4,6},{5,1},{6,4},{7,3},{8,10},{9,13},{10,... | collective-permute-start | bytes 1769480 | tf_op jit(solution)/shard_map/ppermute | solution.py:112
  230.8 38.8 %collective-permute-start.48 = (f32[512,768]{1,0:T(8,128)S(1)}, f32[512,768]{1,0:T(8,128)S(1)}, u32[]{:S(2)}, u32[]{:S(2)}) collective-permute-start(f32[512,768]{1,0:T(8,128)S(1)} %get-tuple-element.391.refs_1_), channel_id=1, source_target_pairs={{0,8},{1,9},{2,10},{3,11},{4,12},{5,13},{6,14},{7,15},{8,0},{9,1},... | collective-permute-start | bytes 4718600 | tf_op jit(solution)/shard_map/ppermute | solution.py:112
  241.1 16.9 %collective-permute-start.47 = (f32[384,768]{1,0:T(8,128)S(1)}, f32[384,768]{1,0:T(8,128)S(1)}, u32[]{:S(2)}, u32[]{:S(2)}) collective-permute-start(f32[384,768]{1,0:T(8,128)S(1)} %get-tuple-element.388.refs_1_), channel_id=1, source_target_pairs={{0,4},{1,3},{2,6},{3,1},{4,0},{5,7},{6,2},{7,5},{8,12},{9,11},{10,... | collective-permute-start | bytes 3538952 | tf_op jit(solution)/shard_map/ppermute | solution.py:112
  252.3 19.7 %collective-permute-start.46 = (f32[384,768]{1,0:T(8,128)S(1)}, f32[384,768]{1,0:T(8,128)S(1)}, u32[]{:S(2)}, u32[]{:S(2)}) collective-permute-start(f32[384,768]{1,0:T(8,128)S(1)} %get-tuple-element.387.refs_1_), channel_id=1, source_target_pairs={{0,4},{1,3},{2,6},{3,1},{4,0},{5,7},{6,2},{7,5},{8,12},{9,11},{10,... | collective-permute-start | bytes 3538952 | tf_op jit(solution)/shard_map/ppermute | solution.py:112
  (38 other events, 385.2 us)
where the time goes:
time: 277 us; the launch traced here: 274 us
  Pallas kernels  103 us (37%)
  waiting for transfers between devices  90.5 us (33%)
  starting transfers between devices  72.7 us (26%)
  local copies, waits for them, and re-layouts  5.1 us (2%)
    pallas_call x69, Pallas kernels, call(): pl.pallas_call(kernel, grid=grid, in_specs=list(in_specs) + [anywhere()]...  103 us
    ppermute x46, waiting for transfers between devices, swap(): return lax.ppermute(v, ('dp', 'tensor'), pairs)  86.9 us
    ppermute x46, starting transfers between devices, swap(): return lax.ppermute(v, ('dp', 'tensor'), pairs)  61 us
    ppermute x5, starting transfers between devices, other(): return lax.ppermute(v, 'tensor', swap)  11.7 us
  transfers between devices with their start and end apart: 51, of which 23 were waited for; matrix products, arithmetic and copies ran while one was open for 0% of the time, Pallas kernels for 33%

commit v1 on v0

--- a/solution.py
+++ b/solution.py
@@ -223,9 +223,6 @@
     scale = HEAD_DIM ** (-0.5)
 
     wq = jnp.transpose(w_qkv, (1, 0, 2))
-    bias3 = jnp.concatenate([qv_bias[0], jnp.zeros((W,), F32), qv_bias[1]]).reshape(1, 3 * W)
-    g1, g2 = ln_gains[0:1], ln_gains[1:2]
-    b1, b2 = ln_biases[0:1], ln_biases[1:2]
     out_b = out_bias.reshape(1, D)
     down_b = down_bias.reshape(1, D)
     up_b = up_bias.reshape(1, FL)
@@ -303,7 +300,7 @@
         off = half * RH
         names = ("a", "qkv", "pr", "ctx", "x_kept")
 
-        def body(len_ref, x_ref, wq_ref, b3_ref, g_ref, b_ref, wo_ref, *rest):
+        def body(len_ref, x_ref, wq_ref, qvb_ref, g_ref, b_ref, wo_ref, *rest):
             part_ref, a_out, qkv_out, pr_out, ctx_out, x_out, a_ref, qkv_ref, pr_ref, ctx_ref, sems = rest[-11:]
             mine = pl.ds(off, RH)
             copies = []
@@ -315,12 +312,15 @@
 
             copy_out(x_ref.at[mine], x_out.at[mine])
             n, _ = normed(x_ref[mine, :].astype(F32))
-            a = (n * g_ref[...] + b_ref[...]).astype(BF16)
+            a = (n * g_ref[0:1] + b_ref[0:1]).astype(BF16)
             a_ref[...] = a
             copy_out(a_ref, a_out.at[mine])
             for c in range(3):
                 cols = pl.ds(c * W, W)
-                qkv_ref[:, cols] = (mm(a, wq_ref[c]) + b3_ref[:, cols]).astype(BF16)
+                v = mm(a, wq_ref[c])
+                if c != 1:
+                    v = v + qvb_ref[c // 2 : c // 2 + 1]
+                qkv_ref[:, cols] = v.astype(BF16)
             copy_out(qkv_ref, qkv_out.at[mine])
             lane = lax.broadcasted_iota(jnp.int32, (SP, 128), 1)
             key_at = lax.broadcasted_iota(jnp.int32, (SP, SP), 0)
@@ -349,7 +349,7 @@
             for copy in copies:
                 copy.wait()
 
-        ins = [caption_lengths, here(state["x"]), wq, bias3, g1, b1, w_out]
+        ins = [in_hbm(caption_lengths), here(state["x"]), wq, in_hbm(qv_bias), in_hbm(ln_gains), in_hbm(ln_biases), w_out]
         specs = [smem()] + [in_vmem()] * 6
         outs = [
             vmem((RH, D), F32),
@@ -398,13 +398,13 @@
             h = x_ref[...].astype(F32) + (p_ref[...] + r_ref[...]) + ob_ref[...]
             h_ref[...] = h.astype(BF16)
             n, _ = normed(h)
-            c = (n * g_ref[...] + b_ref[...]).astype(BF16)
+            c = (n * g_ref[1:2] + b_ref[1:2]).astype(BF16)
             c_ref[...] = c
             ct_ref[...] = c.T
 
         off = half * (steps // 2)
         row = lambda t: (t + off, 0)
-        ins = [state["x"], parts[half], got[half], out_b, g2, b2]
+        ins = [state["x"], parts[half], got[half], out_b, in_hbm(ln_gains), in_hbm(ln_biases)]
         specs = [pl.BlockSpec((BR, D), row), rowD, rowD, in_vmem(), in_vmem(), in_vmem()]
         outs = [vmem((R, D), BF16), vmem((R, D), BF16), vmem((D, R), BF16)]
         out_specs = [
@@ -579,7 +579,7 @@
             step = pl.program_id(0)
             e = e0_ref[...] + e1_ref[...]
             n, inverse = normed(h_ref[...].astype(F32))
-            dh = dy_ref[...].astype(F32) + norm_back(e, n, inverse, g_ref[...])
+            dh = dy_ref[...].astype(F32) + norm_back(e, n, inverse, g_ref[1:2])
             dhr = dh.astype(BF16)
             dh_ref[...] = dhr
             dctx_ref[...] = mm(dhr, wo_ref[...], 1, 1).astype(BF16)
@@ -599,7 +599,7 @@
         state["dh"], state["dctx"], state["go"], state["back2"] = call(
             body,
             (steps,),
-            [here(state["h"]), here(state["dy"]), in_hbm(state["ctx"]), w_out, g2]
+            [here(state["h"]), here(state["dy"]), in_hbm(state["ctx"]), w_out, in_hbm(ln_gains)]
             + [here(state["dc"]), here(state["dc_got"])],
             [rowD, rowD, rowW, in_vmem(), in_vmem(), rowD, rowD],
             [hbm((R, D), BF16), vmem((R, W), BF16), sds((W, D), F32), sds((steps, 3, D), F32)],
@@ -608,8 +608,9 @@
             vmem=10,
         )
 
-    def attn_back():
-        def body(pr_ref, qkv_ref, dctx_ref, dqkv_ref, sum_ref):
+    def attn_back(half):
+        def body(pr_ref, qkv_ref, dctx_ref, *rest):
+            dqkv_ref, sum_ref = rest[-2:]
             lane = lax.broadcasted_iota(jnp.int32, (SP, 128), 1)
             zero = jnp.zeros((SP, 128), BF16)
             for i in range(IB):
@@ -639,13 +640,29 @@
                     dqkv_ref[rows, pl.ds(2 * W + j * 128, 128)] = dv.astype(BF16)
             sum_ref[0] = colsum(dqkv_ref[...].astype(F32))
 
+        off = half * (steps // 2)
+        ins = [in_hbm(state["pr"]), in_hbm(state["qkv"]), here(state["dctx"])]
+        specs = [
+            pl.BlockSpec((IB, heads, SP, SP), lambda t: (t + off, 0, 0, 0)),
+            pl.BlockSpec((BR, 3 * W), lambda t: (t + off, 0)),
+            pl.BlockSpec((BR, W), lambda t: (t + off, 0)),
+        ]
+        aliases = {}
+        if half:
+            aliases = {3: 0, 4: 1}
+            ins += [here(state["dqkv"]), here(state["qkv_sums"])]
+            specs += [anywhere()] * 2
         state["dqkv"], state["qkv_sums"] = call(
             body,
-            (steps,),
-            [in_hbm(state["pr"]), in_hbm(state["qkv"]), here(state["dctx"])],
-            [pl.BlockSpec((IB, heads, SP, SP), lambda t: (t, 0, 0, 0)), row3, rowW],
-            [vmem((R, 3 * W), BF16), sds((steps, 1, 3 * W), F32)],
-            [row3, pl.BlockSpec((1, 1, 3 * W), lambda t: (t, 0, 0))],
+            (steps // 2,),
+            ins,
+            specs,
+            [vmem((R, 3 * W), BF16), vmem((steps, 1, 3 * W), F32)],
+            [
+                pl.BlockSpec((BR, 3 * W), lambda t: (t + off, 0)),
+                pl.BlockSpec((1, 1, 3 * W), lambda t: (t + off, 0, 0)),
+            ],
+            aliases=aliases,
             order=order,
             vmem=8,
         )
@@ -806,7 +823,7 @@
         def body(x_ref, dh_ref, g_ref, e0_ref, e1_ref, o_ref, sum_ref, ys):
             e = e0_ref[...] + e1_ref[...]
             n, inverse = normed(x_ref[...].astype(F32))
-            dx = dh_ref[...].astype(F32) + norm_back(e, n, inverse, g_ref[...])
+            dx = dh_ref[...].astype(F32) + norm_back(e, n, inverse, g_ref[0:1])
             put_rows(ys, dx)
             sum_ref[0, 0:1] = colsum(e * n)
             sum_ref[0, 1:2] = colsum(e)
@@ -815,7 +832,7 @@
         state["grad_tokens"], state["back1"] = call(
             body,
             (steps,),
-            [in_hbm(state["x_kept"]), in_hbm(state["dh"]), g1, here(state["da"]), here(state["da_got"])],
+            [in_hbm(state["x_kept"]), in_hbm(state["dh"]), in_hbm(ln_gains), here(state["da"]), here(state["da_got"])],
             [rowD, rowD, in_vmem(), rowD, rowD],
             [hbm((seq, items, D), BF16), sds((steps, 2, D), F32)],
             [whole((seq, items, D)), pl.BlockSpec((1, 2, D), lambda t: (t, 0, 0))],
@@ -893,7 +910,7 @@
         )
 
     jobs = {
-        "dc": dc, "y": y, "back2": back2, "attn": attn_back, "gqkv": gqkv, "da": da, "back1": back1, "out": out,
+        "dc": dc, "y": y, "back2": back2, "attn": lambda: attn_back(0), "attn2": lambda: attn_back(1), "gqkv": gqkv, "da": da, "back1": back1, "out": out,
         "gather": gather, "small": small, "dc_send": dc_send, "da_send": da_send, "y_send": y_send,
         "qkv_send": lambda: state["qkv_send"](),
     }
@@ -928,12 +945,12 @@
 
 PLAN = {
     "units": (1, 1, 2, 2),
-    "dims": (("yxab", "xyab"), ("yxab", "xyab"), ("ayxb", "axyb"), ("yxab", "xyab"), ("yxab", "xyab"), ("yxab", "xyab")),
+    "dims": (("xyab", "yxab"), ("xyba", "yxba"), ("yxab", "xyab"), ("ayxb", "axyb"), ("yxab", "xyab"), ("yxab", "xyab")),
     "order": (
-        "F0", "F1", "F2", "F3", "0", "dc", "1", "dc_send", "back2", "attn", "3", "1", "0", "gqkv", "qkv_send", "3",
-        "1", "2", "3", "5", "1", "0", "da", "4", "1", "3", "2", "y", "0", "y_send", "4", "5", "2", "3", "da_send",
-        "out", "3", "4", "back1", "2", "5", "1", "4", "2", "gather", "0", "5", "4", "1", "0", "small", "5", "3",
-        "2", "small", "5", "0", "4", "5", "small", "small", "2", "4",
+        "F0", "F1", "F2", "F3", "dc", "0", "1", "dc_send", "back2", "attn", "2", "attn2", "gqkv", "0", "1",
+        "qkv_send", "2", "3", "da", "2", "da_send", "1", "5", "3", "y", "0", "2", "1", "0", "5", "4", "2", "3",
+        "y_send", "back1", "5", "2", "4", "out", "3", "0", "4", "gather", "5", "3", "0", "4", "small", "5", "5",
+        "3", "4", "2", "small", "1", "1", "0", "4", "5", "3", "small", "1", "small", "4",
     ),
 }
 

time: 277 us -> 273 us (0.986)
  waiting for transfers between devices: 90.5 us -> 70.5 us
  Pallas kernels: 103 us -> 117 us
  starting transfers between devices: 72.7 us -> 77.1 us
  local copies, waits for them, and re-layouts: 5.1 us -> 1.83 us
    ppermute x46, waiting for transfers between devices: 86.9 us -> 68.2 us  [swap(): return lax.ppermute(v, ('dp', 'tensor'), pairs)]
    ppermute x46, starting transfers between devices: 61 us -> 76.3 us  [swap(): return lax.ppermute(v, ('dp', 'tensor'), pairs)]
    pallas_call x69 -> x70, Pallas kernels: 103 us -> 117 us  [call(): pl.pallas_call(kernel, grid=grid, in_specs=list(in_specs) + [anywhere()]...]
    ppermute x5, starting transfers between devices: 11.7 us -> 0.78 us  [other(): return lax.ppermute(v, 'tensor', swap)]
  transfers between devices with their start and end apart: 51 -> 51, of which waited for: 23 -> 21; matrix products, arithmetic and copies ran while one was open for 0% -> 0% of each run, Pallas kernels for 33% -> 38%
where the time goes in v1:
time: 273 us; the launch traced here: 269 us
  Pallas kernels  117 us (43%)
  starting transfers between devices  77.1 us (28%)
  waiting for transfers between devices  70.5 us (26%)
    pallas_call x70, Pallas kernels, call(): pl.pallas_call(kernel, grid=grid, in_specs=list(in_specs) + [anywhere()]...  117 us
    ppermute x46, starting transfers between devices, swap(): return lax.ppermute(v, ('dp', 'tensor'), pairs)  76.3 us
    ppermute x46, waiting for transfers between devices, swap(): return lax.ppermute(v, ('dp', 'tensor'), pairs)  68.2 us
  transfers between devices with their start and end apart: 51, of which 21 were waited for; matrix products, arithmetic and copies ran while one was open for 0% of the time, Pallas kernels for 38%

profile of v1, /device:TPU:0, one launch (start us, length us, event | category | flops | bytes accessed | tf_op | source)
XLA Modules:
  0.0 268.8 jit_solution(13775514723691324920)
XLA Ops:
  4.4 6.6 %shard_map.230 = (f32[768,768]{1,0:T(8,128)S(1)}, bf16[1536,768]{1,0:T(8,128)(2,1)}, bf16[1536,1152]{1,0:T(8,128)(2,1)}, bf16[8,6,192,192]{3,2,1,0:T(8,128)(2,1)...) custom-call(s32[8]{0:T(128)} %refs_0_.6, ...), custom_call_target="tpu_custom_call" | custom-call | flops 1024 | bytes 1024 | tf_op jit(solution)/shard_map/pallas_call | solution.py:53
  11.5 6.6 %shard_map.231 = (f32[768,768]{1,0:T(8,128)S(1)}, bf16[1536,768]{1,0:T(8,128)(2,1)}, bf16[1536,1152]{1,0:T(8,128)(2,1)}, bf16[8,6,192,192]{3,2,1,0:T(8,128)(2,1)...) custom-call(s32[8]{0:T(128)} %refs_0_.6, ...), custom_call_target="tpu_custom_call", output_to_operand_aliasing={{1}: (7, {}), {2}: (8, {}), {3}: (9, {}), {4}: (10, {}), {5... | custom-call | flops 1024 | bytes 1024 | tf_op jit(solution)/shard_map/pallas_call | solution.py:53
  18.3 12.8 %shard_map.232 = (bf16[1536,768]{1,0:T(8,128)(2,1)S(1)}, bf16[1536,768]{1,0:T(8,128)(2,1)S(1)}, bf16[768,1536]{1,0:T(8,128)(2,1)S(1)}, f32[8,128]{1,0:T(8,128)}) custom-call(bf16[1536,768]{1,0:T(8,128)(2,1)S(1)} %get-tuple-element.214.refs_1_.refs_0_, f32[768,768]{1,0:T(8,128)S(1)} %get-tuple-element.223.refs_1_, ...), custom_call_target="tpu_custom_call" | custom-call | flops 1024 | bytes 1024 | tf_op jit(solution)/shard_map/pallas_call | solution.py:53
  43.7 5.5 %shard_map.237 = (f32[512,768]{1,0:T(8,128)S(1)}, f32[512,768]{1,0:T(8,128)S(1)}, f32[1,512]{1,0:T(1,128)S(1)}, bf16[1536,512]{1,0:T(8,128)(2,1)S(1)}, bf16[1536,512]{1,0:T(8,128)(2,1)S(1)}, /*index=5*/f32[8,128]{1,0:T(8,128)}) custom-call(s32[1]{0:T(128)} %bitcast.4.refs_5_.refs_0_.refs_1_, bf16[1536,768]{1,0:T(8,128)(2,1)S(1)} %get-tuple-element.231.refs_1_, ...), custom_call_target="tpu_custom_call" | custom-call | flops 1024 | bytes 1024 | tf_op jit(solution)/shard_map/pallas_call | solution.py:53
  49.2 5.9 %shard_map.238 = (f32[512,768]{1,0:T(8,128)S(1)}, f32[512,768]{1,0:T(8,128)S(1)}, f32[1,512]{1,0:T(1,128)S(1)}, bf16[1536,512]{1,0:T(8,128)(2,1)S(1)}, bf16[1536,512]{1,0:T(8,128)(2,1)S(1)}, /*index=5*/f32[8,128]{1,0:T(8,128)}) custom-call(s32[1]{0:T(128)} %bitcast.10.refs_11_.refs_0_, bf16[1536,768]{1,0:T(8,128)(2,1)S(1)} %get-tuple-element.231.refs_1_, ...), custom_call_target="tpu_custom_call" | custom-call | flops 1024 | bytes 1024 | tf_op jit(solution)/shard_map/pallas_call | solution.py:53
  55.1 4.5 %shard_map.239 = (f32[1536,768]{1,0:T(8,128)S(1)}, f32[8,128]{1,0:T(8,128)}) custom-call(bf16[1536,256]{1,0:T(8,128)(2,1)S(1)} %get-tuple-element.249.refs_0_, bf16[1536,256]{1,0:T(8,128)(2,1)S(1)} %get-tuple-element.250.refs_1_, bf16[1536,512]{1,0:T(8,128)(2,1)S(1)} %get-tuple-element.251.refs_2_, bf16[1536,512]{1,0:T(8,128)(2,1)S(1)} %get-tuple-element.252.refs_3_, ...), custom_call_target="tpu_custom_call" | custom-call | flops 1024 | bytes 1024 | tf_op jit(solution)/shard_map/pallas_call | solution.py:53
  67.8 8.5 %shard_map.243 = (bf16[1536,768]{1,0:T(8,128)(2,1)}, bf16[1536,384]{1,0:T(8,128)(2,1)S(1)}, f32[384,768]{1,0:T(8,128)S(1)}, f32[4,3,768]{2,1,0:T(4,128)S(1)}, f32[8,128]{1,0:T(8,128)}) custom-call(bf16[1536,768]{1,0:T(8,128)(2,1)S(1)} %get-tuple-element.230.refs_0_.refs_1_, bf16[1536,768]{1,0:T(8,128)(2,1)S(1)} %get-tuple-element.233.refs_3_.refs_1_, ...), custom_call_target="tpu_custom_call" | custom-call | flops 1024 | bytes 1024 | tf_op jit(solution)/shard_map/pallas_call | solution.py:53
  76.3 6.8 %shard_map.244 = (bf16[1536,1152]{1,0:T(8,128)(2,1)S(1)}, f32[4,1,1152]{2,1,0:T(1,128)S(1)}, f32[8,128]{1,0:T(8,128)}) custom-call(bf16[8,6,192,192]{3,2,1,0:T(8,128)(2,1)} %get-tuple-element.246.refs_0_, bf16[1536,1152]{1,0:T(8,128)(2,1)} %get-tuple-element.247.refs_1_, bf16[1536,384]{1,0:T(8,128)(2,1)S(1)} %get-tuple-element.264.refs_2_, ...), custom_call_target="tpu_custom_call" | custom-call | flops 1024 | bytes 1024 | tf_op jit(solution)/shard_map/pallas_call | solution.py:53
  85.4 7.0 %shard_map.246 = (bf16[1536,1152]{1,0:T(8,128)(2,1)S(1)}, f32[4,1,1152]{2,1,0:T(1,128)S(1)}, f32[8,128]{1,0:T(8,128)}) custom-call(bf16[8,6,192,192]{3,2,1,0:T(8,128)(2,1)} %get-tuple-element.246.refs_0_, bf16[1536,1152]{1,0:T(8,128)(2,1)} %get-tuple-element.247.refs_1_, ...), custom_call_target="tpu_custom_call", output_to_operand_aliasing={{0}: (3, {}), {1}: (4, {})} | custom-call | flops 1024 | bytes 1024 | tf_op jit(solution)/shard_map/pallas_call | solution.py:53
  92.4 5.8 %shard_map.247 = (f32[384,768]{1,0:T(8,128)S(1)}, f32[384,768]{1,0:T(8,128)S(1)}, f32[384,768]{1,0:T(8,128)S(1)}, f32[384,768]{1,0:T(8,128)S(1)}, f32[8,128]{1,0:T(8,128)}) custom-call(s32[1]{0:T(128)} %bitcast.4.refs_5_.refs_0_.refs_1_, s32[1]{0:T(128)} %bitcast.4.refs_5_.refs_0_.refs_1_, bf16[1536,768]{1,0:T(8,128)(2,1)S(1)} %copy-done.3, ...), custom_call_target="tpu_custom_call" | custom-call | flops 1024 | bytes 1024 | tf_op jit(solution)/shard_map/pallas_call | solution.py:53
  106.5 4.4 %shard_map.253 = (f32[1536,768]{1,0:T(8,128)S(1)}, f32[8,128]{1,0:T(8,128)}) custom-call(bf16[1536,1152]{1,0:T(8,128)(2,1)S(1)} %get-tuple-element.273.refs_3_.refs_0_, bf16[3,768,384]{2,1,0:T(8,128)(2,1)S(1)} %bitcast.24, f32[8,128]{1,0:T(8,128)} %get-tuple-element.293.refs_2_), custom_call_target="tpu_custom_call" | custom-call | flops 1024 | bytes 1024 | tf_op jit(solution)/shard_map/pallas_call | solution.py:53
  110.9 4.5 %collective-permute-done.13.refs_1_ = f32[128,768]{1,0:T(8,128)S(1)} collective-permute-done((f32[128,768]{1,0:T(8,128)S(1)}, f32[128,768]{1,0:T(8,128)S(1)}, u32[]{:S(2)}, u32[]{:S(2)}) %collective-permute-start.13) | collective-permute-done | bytes 393248 | tf_op jit(solution)/shard_map/ppermute | solution.py:112
  121.4 4.6 %collective-permute-done.10.refs_2_ = f32[256,768]{1,0:T(8,128)S(1)} collective-permute-done((f32[256,768]{1,0:T(8,128)S(1)}, f32[256,768]{1,0:T(8,128)S(1)}, u32[]{:S(2)}, u32[]{:S(2)}) %collective-permute-start.10) | collective-permute-done | bytes 786464 | tf_op jit(solution)/shard_map/ppermute | solution.py:112
  128.9 4.3 %shard_map.259 = (f32[1536,768]{1,0:T(8,128)S(1)}, f32[8,128]{1,0:T(8,128)}) custom-call(bf16[1536,256]{1,0:T(8,128)(2,1)S(1)} %get-tuple-element.235.refs_0_, bf16[1536,256]{1,0:T(8,128)(2,1)S(1)} %get-tuple-element.237.refs_1_, bf16[1536,512]{1,0:T(8,128)(2,1)S(1)} %get-tuple-element.239.refs_2_, bf16[1536,512]{1,0:T(8,128)(2,1)S(1)} %get-tuple-element.241.refs_3_, ...), custom_call_target="tpu_custom_call" | custom-call | flops 1024 | bytes 1024 | tf_op jit(solution)/shard_map/pallas_call | solution.py:53
  133.3 4.5 %collective-permute-start.20 = (f32[64,768]{1,0:T(8,128)S(1)}, f32[64,768]{1,0:T(8,128)S(1)}, u32[]{:S(2)}, u32[]{:S(2)}) collective-permute-start(f32[64,768]{1,0:T(8,128)S(1)} %get-tuple-element.316.refs_0_), channel_id=1, source_target_pairs={{0,16},{1,17},{2,18},{3,19},{4,20},{5,21},{6,22},{7,23},{8,24},{9,... | collective-permute-start | bytes 589832 | tf_op jit(solution)/shard_map/ppermute | solution.py:112
  151.9 4.8 %collective-permute-start.29 = (f32[128,768]{1,0:T(8,128)S(1)}, f32[128,768]{1,0:T(8,128)S(1)}, u32[]{:S(2)}, u32[]{:S(2)}) collective-permute-start(f32[128,768]{1,0:T(8,128)S(1)} %get-tuple-element.344.refs_0_), channel_id=1, source_target_pairs={{0,16},{1,17},{2,18},{3,19},{4,20},{5,21},{6,22},{7,23},{8,24},{9,... | collective-permute-start | bytes 1179656 | tf_op jit(solution)/shard_map/ppermute | solution.py:112
  156.7 8.5 %shard_map.269 = (bf16[185,8,768]{2,1,0:T(8,128)(2,1)}, f32[4,2,768]{2,1,0:T(2,128)S(1)}, f32[8,128]{1,0:T(8,128)}) custom-call(bf16[1536,768]{1,0:T(8,128)(2,1)} %get-tuple-element.331.refs_0_, bf16[1536,768]{1,0:T(8,128)(2,1)} %get-tuple-element.332.refs_1_, f32[2,768]{1,0:T(2,128)} %refs_2_.1, f32[1536,768]{1,0:T(8,128)S(1)} %get-tuple-element.333.refs_3_, ...), custom_call_target="tpu_custom_call" | custom-call | flops 1024 | bytes 1024 | tf_op jit(solution)/shard_map/pallas_call | solution.py:53
  169.7 5.6 %collective-permute-start.33 = (f32[96,768]{1,0:T(8,128)S(1)}, f32[96,768]{1,0:T(8,128)S(1)}, u32[]{:S(2)}, u32[]{:S(2)}) collective-permute-start(f32[96,768]{1,0:T(8,128)S(1)} %get-tuple-element.351.refs_0_), channel_id=1, source_target_pairs={{0,16},{1,17},{2,18},{3,19},{4,20},{5,21},{6,22},{7,23},{8,24},{9,... | collective-permute-start | bytes 884744 | tf_op jit(solution)/shard_map/ppermute | solution.py:112
  175.3 4.7 %shard_map.273 = (bf16[185,8,768]{2,1,0:T(8,128)(2,1)}, f32[8,128]{1,0:T(8,128)}) custom-call(s32[1]{0:T(128)S(6)} %copy.70.refs_0_, bf16[1536,768]{1,0:T(8,128)(2,1)S(1)} %get-tuple-element.230.refs_0_.refs_1_, f32[1536,768]{1,0:T(8,128)S(1)} %get-tuple-element.325.refs_2_, f32[1536,768]{1,0:T(8,128)S(1)} %collective-permute-done.22.refs_3_, ...), custom_call_target="tpu_custom_call" | custom-call | flops 1024 | bytes 1024 | tf_op jit(solution)/shard_map/pallas_call | solution.py:53
  184.9 4.1 %collective-permute-done.27.refs_1_ = f32[96,768]{1,0:T(8,128)S(1)} collective-permute-done((f32[96,768]{1,0:T(8,128)S(1)}, f32[96,768]{1,0:T(8,128)S(1)}, u32[]{:S(2)}, u32[]{:S(2)}) %collective-permute-start.27) | collective-permute-done | bytes 294944 | tf_op jit(solution)/shard_map/ppermute | solution.py:112
  197.4 7.7 %collective-permute-done.30.refs_1_ = f32[96,768]{1,0:T(8,128)S(1)} collective-permute-done((f32[96,768]{1,0:T(8,128)S(1)}, f32[96,768]{1,0:T(8,128)S(1)}, u32[]{:S(2)}, u32[]{:S(2)}) %collective-permute-start.30) | collective-permute-done | bytes 294944 | tf_op jit(solution)/shard_map/ppermute | solution.py:112
  208.9 6.4 %collective-permute-done.38.refs_2_ = f32[192,768]{1,0:T(8,128)S(1)} collective-permute-done((f32[192,768]{1,0:T(8,128)S(1)}, f32[192,768]{1,0:T(8,128)S(1)}, u32[]{:S(2)}, u32[]{:S(2)}) %collective-permute-start.38) | collective-permute-done | bytes 589856 | tf_op jit(solution)/shard_map/ppermute | solution.py:112
  227.6 5.8 %collective-permute-done.44.refs_2_ = f32[128,768]{1,0:T(8,128)S(1)} collective-permute-done((f32[128,768]{1,0:T(8,128)S(1)}, f32[128,768]{1,0:T(8,128)S(1)}, u32[]{:S(2)}, u32[]{:S(2)}) %collective-permute-start.44) | collective-permute-done | bytes 393248 | tf_op jit(solution)/shard_map/ppermute | solution.py:112
  237.9 14.7 %collective-permute-done.46.refs_2_ = f32[384,768]{1,0:T(8,128)S(1)} collective-permute-done((f32[384,768]{1,0:T(8,128)S(1)}, f32[384,768]{1,0:T(8,128)S(1)}, u32[]{:S(2)}, u32[]{:S(2)}) %collective-permute-start.46) | collective-permute-done | bytes 1179680 | tf_op jit(solution)/shard_map/ppermute | solution.py:112
  (171 shorter events, 111.8 us)
Async XLA Ops:
  37.8 21.8 %collective-permute-start.5 = (f32[256,768]{1,0:T(8,128)S(1)}, f32[256,768]{1,0:T(8,128)S(1)}, u32[]{:S(2)}, u32[]{:S(2)}) collective-permute-start(f32[256,768]{1,0:T(8,128)S(1)} %get-tuple-element.258), channel_id=1, source_target_pairs={{0,2},{1,5},{2,0},{3,7},{4,6},{5,1},{6,4},{7,3},{8,10},{9,13},{10,... | collective-permute-start | bytes 2359304 | tf_op jit(solution)/shard_map/ppermute | solution.py:112
  59.9 23.3 %collective-permute-start.3 = (f32[512,768]{1,0:T(8,128)S(1)}, f32[512,768]{1,0:T(8,128)S(1)}, u32[]{:S(2)}, u32[]{:S(2)}) collective-permute-start(f32[512,768]{1,0:T(8,128)S(1)} %get-tuple-element.245), channel_id=1, source_target_pairs={{0,4},{1,3},{2,6},{3,1},{4,0},{5,7},{6,2},{7,5},{8,12},{9,11},{10,... | collective-permute-start | bytes 4718600 | tf_op jit(solution)/shard_map/ppermute | solution.py:112
  62.0 38.1 %collective-permute-start.2 = (f32[512,768]{1,0:T(8,128)S(1)}, f32[512,768]{1,0:T(8,128)S(1)}, u32[]{:S(2)}, u32[]{:S(2)}) collective-permute-start(f32[512,768]{1,0:T(8,128)S(1)} %get-tuple-element.243), channel_id=1, source_target_pairs={{0,8},{1,9},{2,10},{3,11},{4,12},{5,13},{6,14},{7,15},{8,0},{9,1},... | collective-permute-start | bytes 4718600 | tf_op jit(solution)/shard_map/ppermute | solution.py:112
  63.5 34.7 %collective-permute-start.9 = (f32[128,768]{1,0:T(8,128)S(1)}, f32[128,768]{1,0:T(8,128)S(1)}, u32[]{:S(2)}, u32[]{:S(2)}) collective-permute-start(f32[128,768]{1,0:T(8,128)S(1)} %get-tuple-element.281), channel_id=1, source_target_pairs={{0,4},{1,3},{2,6},{3,1},{4,0},{5,7},{6,2},{7,5},{8,12},{9,11},{10,... | collective-permute-start | bytes 1179656 | tf_op jit(solution)/shard_map/ppermute | solution.py:112
  64.1 34.2 %collective-permute-start.8 = (f32[128,768]{1,0:T(8,128)S(1)}, f32[128,768]{1,0:T(8,128)S(1)}, u32[]{:S(2)}, u32[]{:S(2)}) collective-permute-start(f32[128,768]{1,0:T(8,128)S(1)} %get-tuple-element.279), channel_id=1, source_target_pairs={{0,4},{1,3},{2,6},{3,1},{4,0},{5,7},{6,2},{7,5},{8,12},{9,11},{10,... | collective-permute-start | bytes 1179656 | tf_op jit(solution)/shard_map/ppermute | solution.py:112
  98.4 21.4 %collective-permute-start.11 = (f32[384,768]{1,0:T(8,128)S(1)}, f32[384,768]{1,0:T(8,128)S(1)}, u32[]{:S(2)}, u32[]{:S(2)}) collective-permute-start(f32[384,768]{1,0:T(8,128)S(1)} %get-tuple-element.290), channel_id=1, source_target_pairs={{0,4},{1,3},{2,6},{3,1},{4,0},{5,7},{6,2},{7,5},{8,12},{9,11},{10,... | collective-permute-start | bytes 3538952 | tf_op jit(solution)/shard_map/ppermute | solution.py:112
  100.2 25.7 %collective-permute-start.10 = (f32[256,768]{1,0:T(8,128)S(1)}, f32[256,768]{1,0:T(8,128)S(1)}, u32[]{:S(2)}, u32[]{:S(2)}) collective-permute-start(f32[256,768]{1,0:T(8,128)S(1)} %get-tuple-element.288), channel_id=1, source_target_pairs={{0,4},{1,3},{2,6},{3,1},{4,0},{5,7},{6,2},{7,5},{8,12},{9,11},{10,... | collective-permute-start | bytes 2359304 | tf_op jit(solution)/shard_map/ppermute | solution.py:112
  102.5 43.6 %collective-permute-start.18 = (f32[384,768]{1,0:T(8,128)S(1)}, f32[384,768]{1,0:T(8,128)S(1)}, u32[]{:S(2)}, u32[]{:S(2)}) collective-permute-start(f32[384,768]{1,0:T(8,128)S(1)} %get-tuple-element.313), channel_id=1, source_target_pairs={{0,4},{1,3},{2,6},{3,1},{4,0},{5,7},{6,2},{7,5},{8,12},{9,11},{10,... | collective-permute-start | bytes 3538952 | tf_op jit(solution)/shard_map/ppermute | solution.py:112
  115.5 22.4 %collective-permute-start.15 = (f32[128,768]{1,0:T(8,128)S(1)}, f32[128,768]{1,0:T(8,128)S(1)}, u32[]{:S(2)}, u32[]{:S(2)}) collective-permute-start(f32[128,768]{1,0:T(8,128)S(1)} %get-tuple-element.306.refs_0_), channel_id=1, source_target_pairs={{0,16},{1,17},{2,18},{3,19},{4,20},{5,21},{6,22},{7,23},{8,24},{9,... | collective-permute-start | bytes 1179656 | tf_op jit(solution)/shard_map/ppermute | solution.py:112
  119.9 23.6 %collective-permute-start.19 = (f32[192,768]{1,0:T(8,128)S(1)}, f32[192,768]{1,0:T(8,128)S(1)}, u32[]{:S(2)}, u32[]{:S(2)}) collective-permute-start(f32[192,768]{1,0:T(8,128)S(1)} %get-tuple-element.315), channel_id=1, source_target_pairs={{0,2},{1,5},{2,0},{3,7},{4,6},{5,1},{6,4},{7,3},{8,10},{9,13},{10,... | collective-permute-start | bytes 1769480 | tf_op jit(solution)/shard_map/ppermute | solution.py:112
  149.3 20.4 %collective-permute-start.22 = (f32[1536,768]{1,0:T(8,128)S(1)}, f32[1536,768]{1,0:T(8,128)S(1)}, u32[]{:S(2)}, u32[]{:S(2)}) collective-permute-start(f32[1536,768]{1,0:T(8,128)S(1)} %get-tuple-element.325.refs_2_), channel_id=1, source_target_pairs={{0,1},{1,0},{2,3},{3,2},{4,5},{5,4},{6,7},{7,6},{8,9},{9,8},{10,11... | collective-permute-start | bytes 14155784 | tf_op jit(solution)/shard_map/ppermute | solution.py:236
  149.4 17.0 %collective-permute-start.24 = (f32[256,768]{1,0:T(8,128)S(1)}, f32[256,768]{1,0:T(8,128)S(1)}, u32[]{:S(2)}, u32[]{:S(2)}) collective-permute-start(f32[256,768]{1,0:T(8,128)S(1)} %get-tuple-element.328.refs_1_), channel_id=1, source_target_pairs={{0,2},{1,5},{2,0},{3,7},{4,6},{5,1},{6,4},{7,3},{8,10},{9,13},{10,... | collective-permute-start | bytes 2359304 | tf_op jit(solution)/shard_map/ppermute | solution.py:112
  151.9 28.1 %collective-permute-start.29 = (f32[128,768]{1,0:T(8,128)S(1)}, f32[128,768]{1,0:T(8,128)S(1)}, u32[]{:S(2)}, u32[]{:S(2)}) collective-permute-start(f32[128,768]{1,0:T(8,128)S(1)} %get-tuple-element.344.refs_0_), channel_id=1, source_target_pairs={{0,16},{1,17},{2,18},{3,19},{4,20},{5,21},{6,22},{7,23},{8,24},{9,... | collective-permute-start | bytes 1179656 | tf_op jit(solution)/shard_map/ppermute | solution.py:112
  166.5 52.7 %collective-permute-start.41 = (f32[512,768]{1,0:T(8,128)S(1)}, f32[512,768]{1,0:T(8,128)S(1)}, u32[]{:S(2)}, u32[]{:S(2)}) collective-permute-start(f32[512,768]{1,0:T(8,128)S(1)} %get-tuple-element.377.refs_1_), channel_id=1, source_target_pairs={{0,4},{1,3},{2,6},{3,1},{4,0},{5,7},{6,2},{7,5},{8,12},{9,11},{10,... | collective-permute-start | bytes 4718600 | tf_op jit(solution)/shard_map/ppermute | solution.py:112
  167.8 21.2 %collective-permute-start.27 = (f32[96,768]{1,0:T(8,128)S(1)}, f32[96,768]{1,0:T(8,128)S(1)}, u32[]{:S(2)}, u32[]{:S(2)}) collective-permute-start(f32[96,768]{1,0:T(8,128)S(1)} %get-tuple-element.342), channel_id=1, source_target_pairs={{0,8},{1,9},{2,10},{3,11},{4,12},{5,13},{6,14},{7,15},{8,0},{9,1},... | collective-permute-start | bytes 884744 | tf_op jit(solution)/shard_map/ppermute | solution.py:112
  169.7 21.8 %collective-permute-start.33 = (f32[96,768]{1,0:T(8,128)S(1)}, f32[96,768]{1,0:T(8,128)S(1)}, u32[]{:S(2)}, u32[]{:S(2)}) collective-permute-start(f32[96,768]{1,0:T(8,128)S(1)} %get-tuple-element.351.refs_0_), channel_id=1, source_target_pairs={{0,16},{1,17},{2,18},{3,19},{4,20},{5,21},{6,22},{7,23},{8,24},{9,... | collective-permute-start | bytes 884744 | tf_op jit(solution)/shard_map/ppermute | solution.py:112
  194.2 23.4 %collective-permute-start.35 = (f32[256,768]{1,0:T(8,128)S(1)}, f32[256,768]{1,0:T(8,128)S(1)}, u32[]{:S(2)}, u32[]{:S(2)}) collective-permute-start(f32[256,768]{1,0:T(8,128)S(1)} %get-tuple-element.366.refs_1_), channel_id=1, source_target_pairs={{0,4},{1,3},{2,6},{3,1},{4,0},{5,7},{6,2},{7,5},{8,12},{9,11},{10,... | collective-permute-start | bytes 2359304 | tf_op jit(solution)/shard_map/ppermute | solution.py:112
  206.9 26.5 %collective-permute-start.40 = (f32[256,768]{1,0:T(8,128)S(1)}, f32[256,768]{1,0:T(8,128)S(1)}, u32[]{:S(2)}, u32[]{:S(2)}) collective-permute-start(f32[256,768]{1,0:T(8,128)S(1)} %get-tuple-element.376.refs_1_), channel_id=1, source_target_pairs={{0,2},{1,5},{2,0},{3,7},{4,6},{5,1},{6,4},{7,3},{8,10},{9,13},{10,... | collective-permute-start | bytes 2359304 | tf_op jit(solution)/shard_map/ppermute | solution.py:112
  217.8 18.3 %collective-permute-start.39 = (f32[192,768]{1,0:T(8,128)S(1)}, f32[192,768]{1,0:T(8,128)S(1)}, u32[]{:S(2)}, u32[]{:S(2)}) collective-permute-start(f32[192,768]{1,0:T(8,128)S(1)} %get-tuple-element.375.refs_1_), channel_id=1, source_target_pairs={{0,2},{1,5},{2,0},{3,7},{4,6},{5,1},{6,4},{7,3},{8,10},{9,13},{10,... | collective-permute-start | bytes 1769480 | tf_op jit(solution)/shard_map/ppermute | solution.py:112
  219.2 37.5 %collective-permute-start.48 = (f32[512,768]{1,0:T(8,128)S(1)}, f32[512,768]{1,0:T(8,128)S(1)}, u32[]{:S(2)}, u32[]{:S(2)}) collective-permute-start(f32[512,768]{1,0:T(8,128)S(1)} %get-tuple-element.394.refs_1_), channel_id=1, source_target_pairs={{0,8},{1,9},{2,10},{3,11},{4,12},{5,13},{6,14},{7,15},{8,0},{9,1},... | collective-permute-start | bytes 4718600 | tf_op jit(solution)/shard_map/ppermute | solution.py:112
  225.9 26.7 %collective-permute-start.46 = (f32[384,768]{1,0:T(8,128)S(1)}, f32[384,768]{1,0:T(8,128)S(1)}, u32[]{:S(2)}, u32[]{:S(2)}) collective-permute-start(f32[384,768]{1,0:T(8,128)S(1)} %get-tuple-element.390.refs_1_), channel_id=1, source_target_pairs={{0,4},{1,3},{2,6},{3,1},{4,0},{5,7},{6,2},{7,5},{8,12},{9,11},{10,... | collective-permute-start | bytes 3538952 | tf_op jit(solution)/shard_map/ppermute | solution.py:112
  236.1 30.9 %collective-permute-start.45 = (f32[384,768]{1,0:T(8,128)S(1)}, f32[384,768]{1,0:T(8,128)S(1)}, u32[]{:S(2)}, u32[]{:S(2)}) collective-permute-start(f32[384,768]{1,0:T(8,128)S(1)} %get-tuple-element.389.refs_1_), channel_id=1, source_target_pairs={{0,4},{1,3},{2,6},{3,1},{4,0},{5,7},{6,2},{7,5},{8,12},{9,11},{10,... | collective-permute-start | bytes 3538952 | tf_op jit(solution)/shard_map/ppermute | solution.py:112
  236.2 24.3 %collective-permute-start.50 = (f32[256,768]{1,0:T(8,128)S(1)}, f32[256,768]{1,0:T(8,128)S(1)}, u32[]{:S(2)}, u32[]{:S(2)}) collective-permute-start(f32[256,768]{1,0:T(8,128)S(1)} %get-tuple-element.400.refs_1_), channel_id=1, source_target_pairs={{0,2},{1,5},{2,0},{3,7},{4,6},{5,1},{6,4},{7,3},{8,10},{9,13},{10,... | collective-permute-start | bytes 2359304 | tf_op jit(solution)/shard_map/ppermute | solution.py:112
  237.2 21.9 %collective-permute-start.47 = (f32[16,768]{1,0:T(8,128)S(1)}, f32[16,768]{1,0:T(8,128)S(1)}, u32[]{:S(2)}, u32[]{:S(2)}) collective-permute-start(f32[16,768]{1,0:T(8,128)S(1)} %get-tuple-element.393.refs_0_), channel_id=1, source_target_pairs={{0,8},{1,9},{2,10},{3,11},{4,12},{5,13},{6,14},{7,15},{8,0},{9,1},... | collective-permute-start | bytes 147464 | tf_op jit(solution)/shard_map/ppermute | solution.py:112
  (37 other events, 381.0 us)
